TPU v7x, 128 devices: a whole 4x4x4 slice. The times are simulated.
128 devices in a mesh: wide: 32 (over y, x, core), narrow: 4 (over z).
Axes of the slice: x: 4, y: 4, z: 4, core: 2. Of those that a mesh axis runs over, the one named last changes fastest.
Arguments:
- history: bfloat16 [512, 96, 768], P('wide'), may hold values from -6 to 6
- w_qkv: bfloat16 [768, 2304], replicated, may hold values from -0.21875 to 0.21875
- w_out: bfloat16 [768, 768], replicated, may hold values from -0.21875 to 0.21875
- dest_owner: int32 [512], P('wide'), may hold values from -1 to 31, as said below
- view_start: int32 [512, 4], P('wide', 'narrow'), may hold values from 0 to 32
- view_length: int32 [512, 4], P('wide', 'narrow'), may hold values from 16 to 64, as said below
- block_list: int32 [512, 4, 4, 4], P('wide', 'narrow'), may hold values from -1 to 3, as said below
- positive_offset: int32 [512, 4], P('wide', 'narrow'), may hold values from 1 to 3
Outputs:
- d_history: float32 [512, 96, 768], P('wide', 'narrow')
- d_wqkv: float32 [768, 2304], P(('wide', 'narrow'))
- d_wout: float32 [768, 768], P(('wide', 'narrow'))
Inputs may be any that keep to these rules, and one draw needn't show every extreme that they name: `dest_owner`: every owner along wide encodes exactly 8 accounts; no device hands more than 1 accounts to one owner; a device holds either 16 live accounts or none. `view_length`: each account has a view of 64 events. `block_list`: the list of query block b holds b first, then distinct earlier blocks or -1.
All inputs are finite; a program needn't handle non-finite values.
Results may differ from a plain program's by a relative error of at most 0.023.
Values may be sent and summed in bfloat16 or wider, within the bound.
A program may use at most 128 MiB of HBM per device.

v0:
```python
import jax
import jax.numpy as jnp
from jax import lax
from jax.sharding import PartitionSpec as P

HEAD_DIM = 64
VIEWS = 4
VLEN = 64


norm_epsilon = 1e-06
score_scale = 4.0
sharpness_divisor = 0.1
loss_scale = 512.0


def unit_heads(values):
    return values * lax.rsqrt(jnp.mean(values * values, axis=-1, keepdims=True) + norm_epsilon)


def view_forward(
    tokens, sequence_extents, blocks, w_qkv, w_out, displaced_query_key_value, shift_out
):
    count, span, width = tokens.shape
    head_size = HEAD_DIM
    heads = width // head_size
    nblocks = blocks.shape[1]
    nlist = blocks.shape[2]
    block = span // nblocks
    rows = jnp.arange(span, dtype=jnp.int32)
    live = rows[None, :] < sequence_extents[:, None]
    tokens = jnp.where(live[:, :, None], tokens, jnp.zeros((), tokens.dtype))
    flat = tokens.reshape(count * span, width).astype(jnp.float32)
    normed = (flat * lax.rsqrt(jnp.mean(flat * flat, axis=1, keepdims=True) + norm_epsilon)).astype(
        jnp.bfloat16
    )
    mixed = jnp.dot(normed, w_qkv, preferred_element_type=jnp.float32) + displaced_query_key_value
    mixed = mixed.reshape(count, nblocks, block, 3, heads, head_size)
    query = unit_heads(mixed[:, :, :, 0]).astype(jnp.bfloat16)
    keyval = jnp.concatenate([unit_heads(mixed[:, :, :, 1:2]), mixed[:, :, :, 2:3]], axis=3).astype(
        jnp.bfloat16
    )
    safe = jnp.maximum(blocks, 0)
    picked = jax.vmap(lambda table, ids: table[ids])(keyval, safe)
    picked = picked.reshape(count, nblocks, nlist * block, 2, heads, head_size)
    keys = picked[:, :, :, 0]
    values = picked[:, :, :, 1]
    scores = jnp.einsum("cqihd,cqjhd->cqhij", query, keys, preferred_element_type=jnp.float32) * (
        score_scale / head_size
    )
    inner = jnp.arange(block, dtype=jnp.int32)
    qpos = jnp.arange(nblocks, dtype=jnp.int32)[:, None] * block + inner[None, :]
    kpos = (safe[:, :, :, None] * block + inner).reshape(count, nblocks, nlist * block)
    listed = jnp.broadcast_to((blocks >= 0)[:, :, :, None], (count, nblocks, nlist, block)).reshape(
        count, nblocks, nlist * block
    )
    kexp = kpos[:, :, None, :]
    qexp = qpos[None, :, :, None]
    visibility_mask = (
        listed[:, :, None, :]
        & (kexp <= qexp)
        & ((kexp < sequence_extents[:, None, None, None]) | (kexp == qexp))
    )
    weights = jnp.where(visibility_mask[:, :, None], jnp.exp(scores), 0.0)
    probs = (weights / jnp.sum(weights, axis=-1, keepdims=True)).astype(jnp.bfloat16)
    attended = jnp.einsum("cqhij,cqjhd->cqihd", probs, values, preferred_element_type=jnp.float32)
    attended = attended.astype(jnp.bfloat16).reshape(count * span, width)
    output = jnp.dot(attended, w_out, preferred_element_type=jnp.float32) + shift_out
    resid = flat + output
    share = jnp.where(live, 1.0, 0.0) / sequence_extents[:, None].astype(jnp.float32)
    pooled_history = jnp.sum(resid.reshape(count, span, width) * share[:, :, None], axis=1)
    crop_representation = pooled_history * lax.rsqrt(
        jnp.sum(pooled_history * pooled_history, axis=1, keepdims=True) + norm_epsilon
    )
    return (crop_representation, (normed, attended))


def on_device(
    history, w_qkv, w_out, dest_owner, view_start, view_length, block_list, positive_offset
):
    wide = lax.axis_size("wide")
    narrow_size = lax.axis_size("narrow")
    narrow_index = lax.axis_index("narrow")
    slots_src, hist_len, width = history.shape
    owned = slots_src // 2
    span = VLEN
    capacity = (slots_src + wide - 1) // wide
    boxes = wide * capacity
    nblocks = block_list.shape[2]
    nlist = block_list.shape[3]
    order = jnp.arange(slots_src, dtype=jnp.int32)
    alive = dest_owner >= 0
    earlier = (dest_owner[:, None] == dest_owner[None, :]) & (order[None, :] < order[:, None])
    ranking = jnp.sum(earlier.astype(jnp.int32), axis=1, dtype=jnp.int32)
    target = jnp.where(alive, dest_owner * capacity + ranking, boxes)
    box_index = jnp.arange(boxes, dtype=jnp.int32)
    matches = target[None, :] == box_index[:, None]
    box_live = jnp.any(matches, axis=1)
    box_source = jnp.sum(jnp.where(matches, order[None, :], 0), axis=1, dtype=jnp.int32)
    starts = view_start[:, 0]
    facts = jnp.concatenate(
        [
            alive.astype(jnp.int32)[:, None],
            view_length,
            positive_offset,
            view_start,
            block_list.reshape(slots_src, nblocks * nlist),
        ],
        axis=1,
    )
    box_facts = jnp.where(box_live[:, None], facts[box_source], 0)

    def contiguous_crop(source, start):
        return lax.dynamic_slice(history, (source, start, jnp.int32(0)), (1, span, width))[0]

    outgoing = jax.vmap(contiguous_crop)(box_source, starts[box_source])
    arrived, arrived_facts = (
        lax.all_to_all(
            outgoing.reshape(wide, capacity, span, width),
            "wide",
            split_axis=0,
            concat_axis=0,
            tiled=True,
        ),
        lax.all_to_all(
            box_facts.reshape(wide, capacity, facts.shape[1]),
            "wide",
            split_axis=0,
            concat_axis=0,
            tiled=True,
        ),
    )
    arrived = arrived.reshape(boxes, span, width)
    arrived_facts = arrived_facts.reshape(boxes, facts.shape[1])
    flags = arrived_facts[:, 0]
    place = jnp.cumsum(flags, dtype=jnp.int32) - 1
    local = jnp.arange(owned, dtype=jnp.int32)
    chosen = (place[None, :] == local[:, None]) & (flags[None, :] > 0)
    pick = jnp.sum(jnp.where(chosen, box_index[None, :], 0), axis=1, dtype=jnp.int32)
    views = arrived[pick]
    mine = arrived_facts[pick]
    own_lengths = mine[:, 1]
    own_offsets = mine[:, 2]
    own_blocks = mine[:, 4:].reshape(owned, nblocks, nlist)
    rows_total = owned * span
    zero_mixed = jnp.zeros((rows_total, 3 * width), jnp.float32)
    zero_out = jnp.zeros((rows_total, width), jnp.float32)

    def run(tokens, displaced_query_key_value, shift_out):
        return view_forward(
            tokens, own_lengths, own_blocks, w_qkv, w_out, displaced_query_key_value, shift_out
        )

    crop_representation, pullback, saved = jax.vjp(run, views, zero_mixed, zero_out, has_aux=True)
    collected_entries = lax.all_gather(crop_representation, "narrow", axis=0, tiled=True)
    similarity_matrix = (
        lax.dot_general(
            crop_representation,
            collected_entries,
            (((1,), (1,)), ((), ())),
            precision=lax.Precision.HIGHEST,
        )
        / sharpness_divisor
    )
    columns = jnp.arange(collected_entries.shape[0], dtype=jnp.int32)
    itself = narrow_index * owned + local
    positive = (narrow_index + own_offsets) % VIEWS * owned + local
    weights = jnp.where(columns[None, :] != itself[:, None], jnp.exp(similarity_matrix), 0.0)
    probs = weights / jnp.sum(weights, axis=1, keepdims=True)
    coef = (
        loss_scale
        / sharpness_divisor
        * (probs - jnp.where(columns[None, :] == positive[:, None], 1.0, 0.0))
    )
    d_embed = jnp.dot(coef, collected_entries, precision=lax.Precision.HIGHEST)
    d_keys = lax.dot_general(
        coef, crop_representation, (((0,), (0,)), ((), ())), precision=lax.Precision.HIGHEST
    )
    d_embed = d_embed + lax.psum_scatter(
        d_keys.astype(jnp.bfloat16), "narrow", scatter_dimension=0, tiled=True
    ).astype(jnp.float32)
    d_tokens, g_mixed, g_out = pullback(d_embed)
    normed, attended = saved
    g_mixed = g_mixed.astype(jnp.bfloat16)
    g_out = g_out.astype(jnp.bfloat16)
    share_rows = width // (wide * narrow_size)
    part = lax.slice_in_dim(normed, 0, share_rows * lax.axis_size(("wide", "narrow")), axis=1)
    grad_qkv = lax.psum_scatter(
        lax.dot_general(
            part, g_mixed, (((0,), (0,)), ((), ())), preferred_element_type=jnp.float32
        ),
        ("wide", "narrow"),
        scatter_dimension=0,
        tiled=True,
    )
    part = lax.slice_in_dim(attended, 0, share_rows * lax.axis_size(("wide", "narrow")), axis=1)
    grad_out = lax.psum_scatter(
        lax.dot_general(part, g_out, (((0,), (0,)), ((), ())), preferred_element_type=jnp.float32),
        ("wide", "narrow"),
        scatter_dimension=0,
        tiled=True,
    )

    def place_rows(piece, start):
        return lax.dynamic_update_slice_in_dim(
            jnp.zeros((hist_len, width), jnp.float32), piece.astype(jnp.float32), start, 0
        )

    slot_of = jnp.minimum(target, boxes - 1)
    back = jnp.zeros((boxes, span, width), jnp.bfloat16).at[pick].set(d_tokens)
    returned = lax.all_to_all(
        back.reshape(wide, capacity, span, width), "wide", split_axis=0, concat_axis=0, tiled=True
    ).reshape(boxes, span, width)
    held = jnp.where(alive[:, None, None], returned[slot_of], jnp.zeros((), jnp.bfloat16))
    spread = jax.vmap(place_rows)(held, starts)
    d_history = lax.psum_scatter(
        spread.astype(jnp.bfloat16), "narrow", scatter_dimension=1, tiled=True
    ).astype(jnp.float32)
    return (d_history, grad_qkv, grad_out)


def solution(mesh):
    return jax.shard_map(
        on_device,
        mesh=mesh,
        in_specs=(
            P("wide", None, None),
            P(),
            P(),
            P("wide"),
            P("wide", "narrow"),
            P("wide", "narrow"),
            P("wide", "narrow", None, None),
            P("wide", "narrow"),
        ),
        out_specs=(
            P("wide", "narrow", None),
            P(("wide", "narrow"), None),
            P(("wide", "narrow"), None),
        ),
        check_vma=False,
    )
```

profile of v0, /device:TPU:0, one launch (start us, length us, event | category | flops | bytes accessed | tf_op | source)
XLA Modules:
  0.0 1157.8 jit_solution(14417389291704636875)
XLA Ops:
  15.3 7.5 all-to-all-start
  27.4 11.2 gather_fusion.3
  38.6 5.5 copy.137
  44.1 7.4 all-to-all-start.1
  51.8 5.8 copy.138
  63.5 29.8 %all-to-all-done.1 = bf16[32,1,64,768]{3,2,1,0:T(8,128)(2,1)} async-done(((bf16[32,1,64,768]{3,2,1,0:T(8,128)(2,1)}), bf16[32,1,64,768]{3,2,1,0:T(8,128)(2,1)}, u32[]{:S(2)}, u32[]{:S(2)}) %all-to-all-start.1) | async-done | bytes 3145760 | tf_op jit(solution)/shard_map/all_to_all | solution.py:118
  98.6 3.8 fusion.58
  108.7 10.9 gather_fusion.6
  119.6 6.9 copy.143
  129.5 7.9 fusion.15
  137.5 3.6 fusion.24
  147.1 13.1 %all_gather.3 = f32[32,768]{1,0:T(8,128)S(1)} all-gather(f32[8,768]{1,0:T(8,128)S(1)} %broadcast_multiply_fusion), channel_id=1, replica_groups=mesh['wide'=32,'narrow'=4] {'narrow'}, dimensions={0}, use_global_device_ids=true | all-gather | bytes 122880 | tf_op jit(solution)/shard_map/all_gather | solution.py:155
  163.3 15.5 %reduce-scatter.9.cloned.1.call-done = bf16[8,768]{1,0:T(8,128)(2,1)} async-done(((bf16[32,768]{1,0:T(8,128)(2,1)}), bf16[8,768]{1,0:T(8,128)(2,1)}) %reduce-scatter.9.cloned.1.call-update) | async-done | bytes 12304 | tf_op jit(solution)/shard_map/reduce_scatter | solution.py:179
  181.9 3.9 reshape.550
  185.8 9.0 fusion.11
  194.8 5.6 fusion.13
  200.5 7.3 convert_bitcast_fusion
  207.8 5.4 convert_bitcast_fusion.1
  214.0 6.4 pad_add_fusion
  220.4 16.7 %copy.155 = bf16[8,4,64,2,12,64]{5,2,1,0,4,3:T(8,128)(2,1)} copy(bf16[8,4,64,2,12,64]{2,5,4,1,0,3:T(8,128)(2,1)} %pad_add_fusion) | data formatting | bytes 12582912 | tf_op jit(solution)/shard_map/transpose(jvp())/add_any | solution.py:46
  237.2 11.8 %copy.156 = bf16[128,16,2,12,64]{4,1,3,2,0:T(8,128)(2,1)} copy(bf16[128,16,2,12,64]{4,1,0,3,2:T(8,128)(2,1)} %bitcast.153) | data formatting | bytes 12582912 | tf_op jit(solution)/shard_map/transpose(jvp())/reshape | solution.py:45
  249.7 45.7 %scatter_fusion.1 = bf16[8,4,16,2,12,64]{5,2,4,3,1,0:T(8,128)(2,1)S(1)} fusion(bf16[8,4,16,2,12,64]{5,2,4,3,1,0:T(8,128)(2,1)S(1)} %broadcast_in_dim.245, s32[128]{0:T(128)S(1)} %reshape.647, bf16[128,16,2,12,64]{4,1,3,2,0:T(8,128)(2,1)} %copy.156), kind=kCustom, calls=%fused_computation.8 | custom fusion | flops 3145728 | bytes 18875392 | tf_op jit(solution)/shard_map/transpose(jvp(vmap()))/scatter-add | solution.py:44
  296.3 3.5 fusion.55
  306.2 4.3 copy.158
  310.5 8.4 reshape.552
  318.9 5.1 fusion.22
  330.6 7.4 all-to-all-start.2
  341.7 38.1 %all-to-all-done.2 = bf16[32,1,64,768]{3,2,1,0:T(8,128)(2,1)} async-done(((bf16[32,1,64,768]{3,2,1,0:T(8,128)(2,1)}), bf16[32,1,64,768]{3,2,1,0:T(8,128)(2,1)}, u32[]{:S(2)}, u32[]{:S(2)}) %all-to-all-start.2) | async-done | bytes 3145760 | tf_op jit(solution)/shard_map/all_to_all | solution.py:211
  379.8 3.7 gather_fusion.5
  387.8 148.8 %while.1 = (s32[]{:T(128)}, bf16[16,96,768]{2,1,0:T(8,128)(2,1)}, s32[16,3]{0,1:T(4,128)S(1)}, bf16[16,64,768]{2,1,0:T(8,128)(2,1)}, s32[]{:T(128)}, /*index=5*/s32[3]{0:T(128)S(1)}, s32[]{:T(128)}) while((s32[]{:T(128)}, bf16[16,96,768]{2,1,0:T(8,128)(2,1)}, s32[16,3]{0,1:T(4,128)S(1)}, bf16[16,64,768]{2,1,0:T(8,128)(2,1)}, s32[]{:T(128)}, ...), condition=%wide.while_cond, body=%wide.while_body.sunk | while | flops 49171 | bytes 491699 | solution.py:205
  543.3 4.3 copy.160
  547.6 8.5 convert_element_type.184
  556.1 6.7 fusion.59
  562.8 363.6 %fusion.52 = (f32[8,2304]{1,0:T(8,128)S(1)}, f32[8,768]{1,0:T(8,128)S(1)}) fusion(f32[768,2304]{1,0:T(8,128)} %fusion.59, f32[768,768]{1,0:T(8,128)S(1)} %copy-done.9), kind=kCustom, calls=%all-reduce-scatter.2 | all-reduce-scatter fusion | flops 3145729 | bytes 9535488
  938.2 12.4 %collective-permute-start.54 = (f32[8,768]{1,0:T(8,128)S(1)}, f32[8,768]{1,0:T(8,128)S(1)}, u32[]{:S(2)}, u32[]{:S(2)}) collective-permute-start(f32[8,768]{1,0:T(8,128)S(1)} %get-tuple-element.24), channel_id=1, source_target_pairs={{0,23},{1,24},{2,25},{3,26},{4,27},{5,28},{6,29},{7,30},{8,31},{9,... | collective-permute-start | bytes 73736
  957.3 3.7 collective-permute-start.50
  962.9 3.7 collective-permute-start.48
  972.4 4.4 collective-permute-start.44
  989.7 3.4 collective-permute-start.38
  1002.0 4.3 collective-permute-start.34
  1011.3 5.3 collective-permute-start.29
  1035.2 4.6 collective-permute-start.18
  1039.9 4.3 collective-permute-start.17
  1051.0 3.7 collective-permute-start.12
  1054.7 3.6 collective-permute-start.11
  1068.4 3.4 collective-permute-start.6
  1081.7 4.0 collective-permute-start.2
  1094.1 52.6 %concatenate.27 = f32[262,2304]{1,0:T(8,128)} concatenate(f32[6,2304]{1,0:T(8,128)S(1)} %collective-permute-done.31, f32[8,2304]{1,0:T(8,128)S(1)} %collective-permute-done.30, f32[8,2304]{1,0:T(8,128)S(1)} %collective-permute-done.29, f32[8,2304]{1,0:T(8,128)S(1)} %collective-permute-done.28, f32[8,2304]{1,0:T(8,128)S(1)} %collective-permute-done.27, ...), dimensions={0} | concatenate | bytes 4829184
  (421 shorter events, 333.6 us)
Async XLA Ops:
  15.3 28.8 %all-to-all-start = ((s32[32,1,20]{2,1,0:T(1,128)}), s32[32,1,20]{2,1,0:T(1,128)}, u32[]{:S(2)}, u32[]{:S(2)}) async-start(s32[32,1,20]{2,1,0:T(1,128)} %bitcast.4), calls=%async_computation | async-start | bytes 32768 | tf_op jit(solution)/shard_map/all_to_all | solution.py:125
  44.1 49.2 %all-to-all-start.1 = ((bf16[32,1,64,768]{3,2,1,0:T(8,128)(2,1)}), bf16[32,1,64,768]{3,2,1,0:T(8,128)(2,1)}, u32[]{:S(2)}, u32[]{:S(2)}) async-start(bf16[32,1,64,768]{3,2,1,0:T(8,128)(2,1)} %copy.137), calls=%async_computation.1 | async-start | bytes 6291456 | tf_op jit(solution)/shard_map/all_to_all | solution.py:118
  51.5 127.3 %reduce-scatter.9.cloned.1.call-start = ((), (), s32[]{:S(2)}) async-start(), calls=%async_computation.5 | async-start | bytes 61440 | tf_op jit(solution)/shard_map/reduce_scatter | solution.py:179
  330.6 49.1 %all-to-all-start.2 = ((bf16[32,1,64,768]{3,2,1,0:T(8,128)(2,1)}), bf16[32,1,64,768]{3,2,1,0:T(8,128)(2,1)}, u32[]{:S(2)}, u32[]{:S(2)}) async-start(bf16[32,1,64,768]{3,2,1,0:T(8,128)(2,1)} %bitcast.154), calls=%async_computation.3 | async-start | bytes 6291456 | tf_op jit(solution)/shard_map/all_to_all | solution.py:211
  338.0 810.2 %reduce-scatter.11.cloned.1.call-start = ((), (), s32[]{:S(2)}) async-start(), calls=%async_computation.6 | async-start | bytes 2949120
  932.9 17.6 %collective-permute-start.58 = (f32[8,768]{1,0:T(8,128)S(1)}, f32[8,768]{1,0:T(8,128)S(1)}, u32[]{:S(2)}, u32[]{:S(2)}) collective-permute-start(f32[8,768]{1,0:T(8,128)S(1)} %get-tuple-element.24), channel_id=1, source_target_pairs={{0,27},{1,28},{2,29},{3,30},{4,31},{5,32},{6,33},{7,34},{8,35},{9,... | collective-permute-start | bytes 73736
  934.3 19.5 %collective-permute-start.57 = (f32[8,768]{1,0:T(8,128)S(1)}, f32[8,768]{1,0:T(8,128)S(1)}, u32[]{:S(2)}, u32[]{:S(2)}) collective-permute-start(f32[8,768]{1,0:T(8,128)S(1)} %get-tuple-element.24), channel_id=1, source_target_pairs={{0,26},{1,27},{2,28},{3,29},{4,30},{5,31},{6,32},{7,33},{8,34},{9,... | collective-permute-start | bytes 73736
  935.6 20.4 %collective-permute-start.56 = (f32[8,768]{1,0:T(8,128)S(1)}, f32[8,768]{1,0:T(8,128)S(1)}, u32[]{:S(2)}, u32[]{:S(2)}) collective-permute-start(f32[8,768]{1,0:T(8,128)S(1)} %get-tuple-element.24), channel_id=1, source_target_pairs={{0,25},{1,26},{2,27},{3,28},{4,29},{5,30},{6,31},{7,32},{8,33},{9,... | collective-permute-start | bytes 73736
  936.9 20.5 %collective-permute-start.55 = (f32[8,768]{1,0:T(8,128)S(1)}, f32[8,768]{1,0:T(8,128)S(1)}, u32[]{:S(2)}, u32[]{:S(2)}) collective-permute-start(f32[8,768]{1,0:T(8,128)S(1)} %get-tuple-element.24), channel_id=1, source_target_pairs={{0,24},{1,25},{2,26},{3,27},{4,28},{5,29},{6,30},{7,31},{8,32},{9,... | collective-permute-start | bytes 73736
  938.2 22.8 %collective-permute-start.54 = (f32[8,768]{1,0:T(8,128)S(1)}, f32[8,768]{1,0:T(8,128)S(1)}, u32[]{:S(2)}, u32[]{:S(2)}) collective-permute-start(f32[8,768]{1,0:T(8,128)S(1)} %get-tuple-element.24), channel_id=1, source_target_pairs={{0,23},{1,24},{2,25},{3,26},{4,27},{5,28},{6,29},{7,30},{8,31},{9,... | collective-permute-start | bytes 73736
  950.6 12.4 %collective-permute-start.53 = (f32[8,768]{1,0:T(8,128)S(1)}, f32[8,768]{1,0:T(8,128)S(1)}, u32[]{:S(2)}, u32[]{:S(2)}) collective-permute-start(f32[8,768]{1,0:T(8,128)S(1)} %get-tuple-element.24), channel_id=1, source_target_pairs={{0,22},{1,23},{2,24},{3,25},{4,26},{5,27},{6,28},{7,29},{8,30},{9,... | collective-permute-start | bytes 73736
  953.8 12.9 %collective-permute-start.52 = (f32[8,768]{1,0:T(8,128)S(1)}, f32[8,768]{1,0:T(8,128)S(1)}, u32[]{:S(2)}, u32[]{:S(2)}) collective-permute-start(f32[8,768]{1,0:T(8,128)S(1)} %get-tuple-element.24), channel_id=1, source_target_pairs={{0,21},{1,22},{2,23},{3,24},{4,25},{5,26},{6,27},{7,28},{8,29},{9,... | collective-permute-start | bytes 73736
  956.0 13.2 %collective-permute-start.51 = (f32[8,768]{1,0:T(8,128)S(1)}, f32[8,768]{1,0:T(8,128)S(1)}, u32[]{:S(2)}, u32[]{:S(2)}) collective-permute-start(f32[8,768]{1,0:T(8,128)S(1)} %get-tuple-element.24), channel_id=1, source_target_pairs={{0,20},{1,21},{2,22},{3,23},{4,24},{5,25},{6,26},{7,27},{8,28},{9,... | collective-permute-start | bytes 73736
  957.3 13.2 %collective-permute-start.50 = (f32[8,768]{1,0:T(8,128)S(1)}, f32[8,768]{1,0:T(8,128)S(1)}, u32[]{:S(2)}, u32[]{:S(2)}) collective-permute-start(f32[8,768]{1,0:T(8,128)S(1)} %get-tuple-element.24), channel_id=1, source_target_pairs={{0,19},{1,20},{2,21},{3,22},{4,23},{5,24},{6,25},{7,26},{8,27},{9,... | collective-permute-start | bytes 73736
  961.0 11.4 collective-permute-start.49
  962.9 13.9 %collective-permute-start.48 = (f32[8,768]{1,0:T(8,128)S(1)}, f32[8,768]{1,0:T(8,128)S(1)}, u32[]{:S(2)}, u32[]{:S(2)}) collective-permute-start(f32[8,768]{1,0:T(8,128)S(1)} %get-tuple-element.24), channel_id=1, source_target_pairs={{0,17},{1,18},{2,19},{3,20},{4,21},{5,22},{6,23},{7,24},{8,25},{9,... | collective-permute-start | bytes 73736
  966.7 12.4 %collective-permute-start.47 = (f32[8,768]{1,0:T(8,128)S(1)}, f32[8,768]{1,0:T(8,128)S(1)}, u32[]{:S(2)}, u32[]{:S(2)}) collective-permute-start(f32[8,768]{1,0:T(8,128)S(1)} %get-tuple-element.24), channel_id=1, source_target_pairs={{0,16},{1,17},{2,18},{3,19},{4,20},{5,21},{6,22},{7,23},{8,24},{9,... | collective-permute-start | bytes 73736
  969.2 13.3 %collective-permute-start.46 = (f32[8,768]{1,0:T(8,128)S(1)}, f32[8,768]{1,0:T(8,128)S(1)}, u32[]{:S(2)}, u32[]{:S(2)}) collective-permute-start(f32[8,768]{1,0:T(8,128)S(1)} %get-tuple-element.24), channel_id=1, source_target_pairs={{0,15},{1,16},{2,17},{3,18},{4,19},{5,20},{6,21},{7,22},{8,23},{9,... | collective-permute-start | bytes 73736
  970.6 13.8 %collective-permute-start.45 = (f32[8,768]{1,0:T(8,128)S(1)}, f32[8,768]{1,0:T(8,128)S(1)}, u32[]{:S(2)}, u32[]{:S(2)}) collective-permute-start(f32[8,768]{1,0:T(8,128)S(1)} %get-tuple-element.24), channel_id=1, source_target_pairs={{0,14},{1,15},{2,16},{3,17},{4,18},{5,19},{6,20},{7,21},{8,22},{9,... | collective-permute-start | bytes 73736
  972.4 14.5 %collective-permute-start.44 = (f32[8,768]{1,0:T(8,128)S(1)}, f32[8,768]{1,0:T(8,128)S(1)}, u32[]{:S(2)}, u32[]{:S(2)}) collective-permute-start(f32[8,768]{1,0:T(8,128)S(1)} %get-tuple-element.24), channel_id=1, source_target_pairs={{0,13},{1,14},{2,15},{3,16},{4,17},{5,18},{6,19},{7,20},{8,21},{9,... | collective-permute-start | bytes 73736
  976.8 12.9 %collective-permute-start.43 = (f32[8,768]{1,0:T(8,128)S(1)}, f32[8,768]{1,0:T(8,128)S(1)}, u32[]{:S(2)}, u32[]{:S(2)}) collective-permute-start(f32[8,768]{1,0:T(8,128)S(1)} %get-tuple-element.24), channel_id=1, source_target_pairs={{0,12},{1,13},{2,14},{3,15},{4,16},{5,17},{6,18},{7,19},{8,20},{9,... | collective-permute-start | bytes 73736
  979.1 14.1 %collective-permute-start.42 = (f32[8,768]{1,0:T(8,128)S(1)}, f32[8,768]{1,0:T(8,128)S(1)}, u32[]{:S(2)}, u32[]{:S(2)}) collective-permute-start(f32[8,768]{1,0:T(8,128)S(1)} %get-tuple-element.24), channel_id=1, source_target_pairs={{0,11},{1,12},{2,13},{3,14},{4,15},{5,16},{6,17},{7,18},{8,19},{9,... | collective-permute-start | bytes 73736
  982.5 12.0 %collective-permute-start.41 = (f32[8,768]{1,0:T(8,128)S(1)}, f32[8,768]{1,0:T(8,128)S(1)}, u32[]{:S(2)}, u32[]{:S(2)}) collective-permute-start(f32[8,768]{1,0:T(8,128)S(1)} %get-tuple-element.24), channel_id=1, source_target_pairs={{0,10},{1,11},{2,12},{3,13},{4,14},{5,15},{6,16},{7,17},{8,18},{9,... | collective-permute-start | bytes 73736
  984.3 11.4 collective-permute-start.40
  989.7 10.8 collective-permute-start.38
  993.1 29.7 %collective-permute-start.30 = (f32[8,2304]{1,0:T(8,128)S(1)}, f32[8,2304]{1,0:T(8,128)S(1)}, u32[]{:S(2)}, u32[]{:S(2)}) collective-permute-start(f32[8,2304]{1,0:T(8,128)S(1)} %get-tuple-element.23), channel_id=1, source_target_pairs={{0,31},{1,32},{2,33},{3,34},{4,35},{5,36},{6,37},{7,38},{8,39},{9,... | collective-permute-start | bytes 221192
  994.5 25.0 %collective-permute-start.31 = (f32[6,2304]{1,0:T(8,128)S(1)}, f32[6,2304]{1,0:T(8,128)S(1)}, u32[]{:S(2)}, u32[]{:S(2)}) collective-permute-start(f32[6,2304]{1,0:T(8,128)S(1)} %slice.80), channel_id=1, source_target_pairs={{0,32},{1,33},{2,34},{3,35},{4,36},{5,37},{6,38},{7,39},{8,40},{9,... | collective-permute-start | bytes 165896
  1011.3 13.2 %collective-permute-start.29 = (f32[8,2304]{1,0:T(8,128)S(1)}, f32[8,2304]{1,0:T(8,128)S(1)}, u32[]{:S(2)}, u32[]{:S(2)}) collective-permute-start(f32[8,2304]{1,0:T(8,128)S(1)} %get-tuple-element.23), channel_id=1, source_target_pairs={{0,30},{1,31},{2,32},{3,33},{4,34},{5,35},{6,36},{7,37},{8,38},{9,... | collective-permute-start | bytes 221192
  1027.1 12.8 %collective-permute-start.22 = (f32[8,2304]{1,0:T(8,128)S(1)}, f32[8,2304]{1,0:T(8,128)S(1)}, u32[]{:S(2)}, u32[]{:S(2)}) collective-permute-start(f32[8,2304]{1,0:T(8,128)S(1)} %get-tuple-element.23), channel_id=1, source_target_pairs={{0,23},{1,24},{2,25},{3,26},{4,27},{5,28},{6,29},{7,30},{8,31},{9,... | collective-permute-start | bytes 221192
  1028.5 15.7 %collective-permute-start.21 = (f32[8,2304]{1,0:T(8,128)S(1)}, f32[8,2304]{1,0:T(8,128)S(1)}, u32[]{:S(2)}, u32[]{:S(2)}) collective-permute-start(f32[8,2304]{1,0:T(8,128)S(1)} %get-tuple-element.23), channel_id=1, source_target_pairs={{0,22},{1,23},{2,24},{3,25},{4,26},{5,27},{6,28},{7,29},{8,30},{9,... | collective-permute-start | bytes 221192
  1031.8 15.1 %collective-permute-start.20 = (f32[8,2304]{1,0:T(8,128)S(1)}, f32[8,2304]{1,0:T(8,128)S(1)}, u32[]{:S(2)}, u32[]{:S(2)}) collective-permute-start(f32[8,2304]{1,0:T(8,128)S(1)} %get-tuple-element.23), channel_id=1, source_target_pairs={{0,21},{1,22},{2,23},{3,24},{4,25},{5,26},{6,27},{7,28},{8,29},{9,... | collective-permute-start | bytes 221192
  1033.9 14.2 %collective-permute-start.19 = (f32[8,2304]{1,0:T(8,128)S(1)}, f32[8,2304]{1,0:T(8,128)S(1)}, u32[]{:S(2)}, u32[]{:S(2)}) collective-permute-start(f32[8,2304]{1,0:T(8,128)S(1)} %get-tuple-element.23), channel_id=1, source_target_pairs={{0,20},{1,21},{2,22},{3,23},{4,24},{5,25},{6,26},{7,27},{8,28},{9,... | collective-permute-start | bytes 221192
  1035.2 14.2 %collective-permute-start.18 = (f32[8,2304]{1,0:T(8,128)S(1)}, f32[8,2304]{1,0:T(8,128)S(1)}, u32[]{:S(2)}, u32[]{:S(2)}) collective-permute-start(f32[8,2304]{1,0:T(8,128)S(1)} %get-tuple-element.23), channel_id=1, source_target_pairs={{0,19},{1,20},{2,21},{3,22},{4,23},{5,24},{6,25},{7,26},{8,27},{9,... | collective-permute-start | bytes 221192
  1039.9 11.1 collective-permute-start.17
  1046.9 11.4 collective-permute-start.15
  1048.2 13.5 %collective-permute-start.14 = (f32[8,2304]{1,0:T(8,128)S(1)}, f32[8,2304]{1,0:T(8,128)S(1)}, u32[]{:S(2)}, u32[]{:S(2)}) collective-permute-start(f32[8,2304]{1,0:T(8,128)S(1)} %get-tuple-element.23), channel_id=1, source_target_pairs={{0,15},{1,16},{2,17},{3,18},{4,19},{5,20},{6,21},{7,22},{8,23},{9,... | collective-permute-start | bytes 221192
  1049.5 13.9 %collective-permute-start.13 = (f32[8,2304]{1,0:T(8,128)S(1)}, f32[8,2304]{1,0:T(8,128)S(1)}, u32[]{:S(2)}, u32[]{:S(2)}) collective-permute-start(f32[8,2304]{1,0:T(8,128)S(1)} %get-tuple-element.23), channel_id=1, source_target_pairs={{0,14},{1,15},{2,16},{3,17},{4,18},{5,19},{6,20},{7,21},{8,22},{9,... | collective-permute-start | bytes 221192
  1051.0 14.5 %collective-permute-start.12 = (f32[8,2304]{1,0:T(8,128)S(1)}, f32[8,2304]{1,0:T(8,128)S(1)}, u32[]{:S(2)}, u32[]{:S(2)}) collective-permute-start(f32[8,2304]{1,0:T(8,128)S(1)} %get-tuple-element.23), channel_id=1, source_target_pairs={{0,13},{1,14},{2,15},{3,16},{4,17},{5,18},{6,19},{7,20},{8,21},{9,... | collective-permute-start | bytes 221192
  1054.7 13.6 %collective-permute-start.11 = (f32[8,2304]{1,0:T(8,128)S(1)}, f32[8,2304]{1,0:T(8,128)S(1)}, u32[]{:S(2)}, u32[]{:S(2)}) collective-permute-start(f32[8,2304]{1,0:T(8,128)S(1)} %get-tuple-element.23), channel_id=1, source_target_pairs={{0,12},{1,13},{2,14},{3,15},{4,16},{5,17},{6,18},{7,19},{8,20},{9,... | collective-permute-start | bytes 221192
  1058.3 13.5 %collective-permute-start.10 = (f32[8,2304]{1,0:T(8,128)S(1)}, f32[8,2304]{1,0:T(8,128)S(1)}, u32[]{:S(2)}, u32[]{:S(2)}) collective-permute-start(f32[8,2304]{1,0:T(8,128)S(1)} %get-tuple-element.23), channel_id=1, source_target_pairs={{0,11},{1,12},{2,13},{3,14},{4,15},{5,16},{6,17},{7,18},{8,19},{9,... | collective-permute-start | bytes 221192
  1061.7 15.2 %collective-permute-start.9 = (f32[8,2304]{1,0:T(8,128)S(1)}, f32[8,2304]{1,0:T(8,128)S(1)}, u32[]{:S(2)}, u32[]{:S(2)}) collective-permute-start(f32[8,2304]{1,0:T(8,128)S(1)} %get-tuple-element.23), channel_id=1, source_target_pairs={{0,10},{1,11},{2,12},{3,13},{4,14},{5,15},{6,16},{7,17},{8,18},{9,... | collective-permute-start | bytes 221192
  1063.4 16.4 %collective-permute-start.8 = (f32[8,2304]{1,0:T(8,128)S(1)}, f32[8,2304]{1,0:T(8,128)S(1)}, u32[]{:S(2)}, u32[]{:S(2)}) collective-permute-start(f32[8,2304]{1,0:T(8,128)S(1)} %get-tuple-element.23), channel_id=1, source_target_pairs={{0,9},{1,10},{2,11},{3,12},{4,13},{5,14},{6,15},{7,16},{8,17},{9,1... | collective-permute-start | bytes 221192
  1065.5 16.1 %collective-permute-start.7 = (f32[8,2304]{1,0:T(8,128)S(1)}, f32[8,2304]{1,0:T(8,128)S(1)}, u32[]{:S(2)}, u32[]{:S(2)}) collective-permute-start(f32[8,2304]{1,0:T(8,128)S(1)} %get-tuple-element.23), channel_id=1, source_target_pairs={{0,8},{1,9},{2,10},{3,11},{4,12},{5,13},{6,14},{7,15},{8,16},{9,17... | collective-permute-start | bytes 221192
  1068.4 17.3 %collective-permute-start.6 = (f32[8,2304]{1,0:T(8,128)S(1)}, f32[8,2304]{1,0:T(8,128)S(1)}, u32[]{:S(2)}, u32[]{:S(2)}) collective-permute-start(f32[8,2304]{1,0:T(8,128)S(1)} %get-tuple-element.23), channel_id=1, source_target_pairs={{0,7},{1,8},{2,9},{3,10},{4,11},{5,12},{6,13},{7,14},{8,15},{9,16}... | collective-permute-start | bytes 221192
  1071.8 16.8 %collective-permute-start.5 = (f32[8,2304]{1,0:T(8,128)S(1)}, f32[8,2304]{1,0:T(8,128)S(1)}, u32[]{:S(2)}, u32[]{:S(2)}) collective-permute-start(f32[8,2304]{1,0:T(8,128)S(1)} %get-tuple-element.23), channel_id=1, source_target_pairs={{0,6},{1,7},{2,8},{3,9},{4,10},{5,11},{6,12},{7,13},{8,14},{9,15},... | collective-permute-start | bytes 221192
  1076.9 15.8 %collective-permute-start.4 = (f32[8,2304]{1,0:T(8,128)S(1)}, f32[8,2304]{1,0:T(8,128)S(1)}, u32[]{:S(2)}, u32[]{:S(2)}) collective-permute-start(f32[8,2304]{1,0:T(8,128)S(1)} %get-tuple-element.23), channel_id=1, source_target_pairs={{0,5},{1,6},{2,7},{3,8},{4,9},{5,10},{6,11},{7,12},{8,13},{9,14},{... | collective-permute-start | bytes 221192
  1079.8 13.0 %collective-permute-start.3 = (f32[8,2304]{1,0:T(8,128)S(1)}, f32[8,2304]{1,0:T(8,128)S(1)}, u32[]{:S(2)}, u32[]{:S(2)}) collective-permute-start(f32[8,2304]{1,0:T(8,128)S(1)} %get-tuple-element.23), channel_id=1, source_target_pairs={{0,4},{1,5},{2,6},{3,7},{4,8},{5,9},{6,10},{7,11},{8,12},{9,13},{1... | collective-permute-start | bytes 221192
  1081.7 11.1 collective-permute-start.2
  (70 other events, 816.1 us)
Sparse Core Ops, SparseCore 0:
  161.7 17.1 reduce-scatter.8
  540.0 27.2 reduce-scatter.10
where the time goes:
time: 1180 us; the launch traced here: 1160 us
  blocking collectives  377 us (32%)
  local copies, waits for them, and re-layouts  256 us (22%)
  starting transfers between devices  183 us (16%)
  other arithmetic  179 us (15%)
  waiting for transfers between devices  83.5 us (7%)
  matrix products  62.7 us (5%)
  between operations  16.3 us (1%)
    unnamed x1, blocking collectives  364 us
    unnamed x65, starting transfers between devices  160 us
    scatter x32, other arithmetic  90.7 us
    unnamed x112, local copies, waits for them, and re-layouts  78.2 us
    scatter x48, local copies, waits for them, and re-layouts  57.8 us
    scatter-add x1, other arithmetic, view_forward(): picked = jax.vmap(lambda table, ids: table[ids])(keyval, safe)  45.7 us
    all_to_all x1, waiting for transfers between devices, on_device(): lax.all_to_all(back.reshape(wide, capacity, span, width), 'wide', split_a...  38.1 us
    all_to_all x1, waiting for transfers between devices, on_device(): lax.all_to_all(outgoing.reshape(wide, capacity, span, width), 'wide', spl...  29.8 us
  transfers between devices with their start and end apart: 69, of which 3 were waited for; matrix products, arithmetic and copies ran while one was open for 42% of the time, Pallas kernels for 0%

commit v1 on v0

v1 whole, which is shorter than its diff:
```python
import functools

import jax
import jax.numpy as jnp
from jax import lax
from jax.experimental import pallas as pl
from jax.experimental.pallas import tpu as pltpu
from jax.sharding import PartitionSpec as P

BF = jnp.bfloat16
F32 = jnp.float32
I32 = jnp.int32
MESH = pl.DeviceIdType.MESH

WIDE = 32
NARROW = 4
CHIP_X = 4
CHIP_Y = 4
OWNED = 8
SLOTS = 16
D = 768
HEAD = 64
SPAN = 64
HIST = 96
GROUP = 256
ROWS = OWNED * SPAN
QROWS = HIST // 2
QCOLS = D // 2
ORROWS = HIST // NARROW
WROWS = D // WIDE
WCOLS = 4 * D
HALF = WCOLS // 2

LIVE, LEN, OFF, START, SLOT, BLOCKS = 0, 1, 2, 3, 4, 5
EPS = 1e-06
VMEM_LIMIT = 60 * 1024 * 1024


def mm(a, b):
    return jnp.dot(a, b, preferred_element_type=F32)


def mm_t(a, b):
    return lax.dot_general(a, b, (((1,), (1,)), ((), ())), preferred_element_type=F32)


def mm_l(a, b):
    return lax.dot_general(a, b, (((0,), (0,)), ((), ())), preferred_element_type=F32)


def split_hi_lo(x):
    hi = x.astype(BF)
    return hi, (x - hi.astype(F32)).astype(BF)


def iota(shape, dim):
    return lax.broadcasted_iota(I32, shape, dim)


def head_diag():
    shape = (GROUP, GROUP)
    return (iota(shape, 0) // HEAD) == (iota(shape, 1) // HEAD)


def spread_heads(x, diag):
    return jnp.where(diag, jnp.concatenate([x, x, x, x], axis=0), jnp.zeros((), x.dtype))


def gather_heads(full, diag):
    kept = jnp.where(diag, full, 0.0)
    return (kept[0:64] + kept[64:128]) + (kept[128:192] + kept[192:256])


def two_rows(x):
    hi = x.astype(BF).astype(F32)
    row = iota((8, GROUP), 0)
    return jnp.where(row == 0, hi, jnp.where(row == 1, x - hi, 0.0)).astype(BF)


def dispatch_kernel(
    msg_s, msg_v, hist, out, facts8, place, hbuf, sbuf, rbuf, frecv, fsm,
    lsem, fsem, bsend, brecv, fsend, frsem, zsend, zrecv,
):
    w = lax.axis_index("wide")
    z = lax.axis_index("narrow")
    load = pltpu.make_async_copy(
        hist.at[:, pl.ds(QROWS * (z // 2), QROWS), pl.ds(QCOLS * (z % 2), QCOLS)], hbuf, lsem
    )
    load.start()
    barrier = pltpu.get_barrier_semaphore()

    def greet(k, c):
        pl.semaphore_signal(barrier, inc=1, device_id=((w + k) % WIDE, z), device_id_type=MESH)
        return c

    lax.fori_loop(1, WIDE, greet, 0)
    for k in range(1, NARROW):
        pl.semaphore_signal(barrier, inc=1, device_id=(w, (z + k) % NARROW), device_id_type=MESH)
    pl.semaphore_wait(barrier, WIDE - 1 + NARROW - 1)

    def fact_copy(k):
        d = (w + k) % WIDE
        return pltpu.make_async_remote_copy(
            src_ref=msg_v.at[d], dst_ref=frecv.at[w], send_sem=fsend.at[k], recv_sem=frsem.at[k],
            device_id=(d, z), device_id_type=MESH,
        )

    def fact_arrival(k):
        s = (w + WIDE - k) % WIDE
        return pltpu.make_async_remote_copy(
            src_ref=msg_v.at[s], dst_ref=frecv.at[s], send_sem=fsend.at[k], recv_sem=frsem.at[k],
            device_id=(s, z), device_id_type=MESH,
        )

    def box_copy(k):
        d = (w + k) % WIDE
        return pltpu.make_async_remote_copy(
            src_ref=sbuf.at[k], dst_ref=rbuf.at[w], send_sem=bsend.at[k], recv_sem=brecv.at[k],
            device_id=(d, z), device_id_type=MESH,
        )

    def box_arrival(k):
        s = (w + WIDE - k) % WIDE
        return pltpu.make_async_remote_copy(
            src_ref=sbuf.at[k], dst_ref=rbuf.at[s], send_sem=bsend.at[k], recv_sem=brecv.at[k],
            device_id=(s, z), device_id_type=MESH,
        )

    def send_facts(k, c):
        fact_copy(k).start()
        return c

    lax.fori_loop(1, WIDE, send_facts, 0)
    load.wait()

    def send_box(k, c):
        sbuf[k] = hbuf[msg_s[(w + k) % WIDE, SLOT]]
        box_copy(k).start()
        return c

    lax.fori_loop(1, WIDE, send_box, 0)
    rbuf[w] = hbuf[msg_s[w, SLOT]]
    frecv[w] = msg_v[w]

    def wait_facts(k, c):
        fact_arrival(k).wait_recv()
        return c

    lax.fori_loop(1, WIDE, wait_facts, 0)
    down = pltpu.make_async_copy(frecv, fsm, fsem)
    down.start()
    down.wait()

    def scan(s, c):
        count, picks = c
        live = fsm[s, 0, LIVE]
        place[s] = jnp.minimum(count, OWNED - 1)
        picks = tuple(
            jnp.where((live > 0) & (count == p), s, picks[p]) for p in range(OWNED)
        )
        return count + live, picks

    _, picks = lax.fori_loop(
        0, WIDE, scan, (jnp.int32(0), tuple(jnp.int32(0) for _ in range(OWNED)))
    )
    for p in range(OWNED):
        facts8[p] = frecv[picks[p]]

    def wait_box(k, c):
        box_arrival(k).wait_recv()
        return c

    lax.fori_loop(1, WIDE, wait_box, 0)
    for p in range(OWNED):
        out[z, p] = rbuf[picks[p]]

    right = (z + 1) % NARROW
    left = (z + 3) % NARROW
    opposite = (z + 2) % NARROW
    part = OWNED // 2

    def hop(quarter, lo, size, to, n):
        where = out.at[quarter, pl.ds(lo, size)]
        return pltpu.make_async_remote_copy(
            src_ref=where, dst_ref=where, send_sem=zsend.at[n], recv_sem=zrecv.at[n],
            device_id=(w, to), device_id_type=MESH,
        )

    to_right = [hop(z, 0, part, right, 0), hop(z, part, part, right, 1)]
    to_left = [hop(z, part, part, left, 2), hop(z, 0, part, left, 3)]
    to_right[0].start()
    to_left[0].start()
    to_right[1].start()
    to_left[1].start()
    hop(left, 0, part, left, 0).wait_recv()
    on_right = hop(left, 0, part, right, 4)
    on_right.start()
    hop(right, part, part, right, 2).wait_recv()
    on_left = hop(right, part, part, left, 5)
    on_left.start()
    hop(left, part, part, left, 1).wait_recv()
    hop(right, 0, part, right, 3).wait_recv()
    hop(opposite, 0, part, left, 4).wait_recv()
    hop(opposite, part, part, right, 5).wait_recv()
    for copy in to_right + to_left + [on_right, on_left]:
        copy.wait_send()

    def drain(k, c):
        fact_copy(k).wait_send()
        box_copy(k).wait_send()
        return c

    lax.fori_loop(1, WIDE, drain, 0)


def forward_kernel(
    facts, hist, wqkv, wout, normed, qkv, inv_heads, inv_tokens, probs, pooled, mean_att
):
    diag = head_diag()
    ones = jnp.where(diag, 1.0, 0.0).astype(BF)
    row48 = iota((SPAN, QROWS), 0)
    col48 = iota((SPAN, QROWS), 1)
    for p in range(OWNED):
        start = facts[p, START]
        length = facts[p, LEN]
        rows = pl.ds(p * SPAN, SPAN)
        source = row48 + start
        alive = row48 < length
        top = jnp.where((col48 == source) & alive, 1.0, 0.0).astype(BF)
        low = jnp.where((col48 + QROWS == source) & alive, 1.0, 0.0).astype(BF)
        left = mm(top, hist[0, p]) + mm(low, hist[2, p])
        right = mm(top, hist[1, p]) + mm(low, hist[3, p])
        square = jnp.sum(left * left, axis=1, keepdims=True) + jnp.sum(
            right * right, axis=1, keepdims=True
        )
        inv = lax.rsqrt(square * (1.0 / D) + EPS)
        normed[rows, 0:QCOLS] = (left * inv).astype(BF)
        normed[rows, QCOLS:D] = (right * inv).astype(BF)
        inv_tokens[rows, :] = jnp.broadcast_to(inv, (SPAN, 128))
        scale = length.astype(F32)
        pooled[p : p + 1, 0:QCOLS] = jnp.sum(left, axis=0, keepdims=True) / scale
        pooled[p : p + 1, QCOLS:D] = jnp.sum(right, axis=0, keepdims=True) / scale
    for j in range(9):
        cols = pl.ds(j * GROUP, GROUP)
        mixed = mm(normed[...], wqkv[:, cols])
        if j < 6:
            square = mm((mixed * mixed).astype(BF), ones)
            inv = lax.rsqrt(square * (1.0 / HEAD) + EPS)
            qkv[:, cols] = (mixed * inv).astype(BF)
            inv_heads[:, cols] = inv.astype(BF)
        else:
            qkv[:, cols] = mixed.astype(BF)

    def one_view(p, c):
        rows = pl.ds(pl.multiple_of(p * SPAN, SPAN), SPAN)
        length = facts[p, LEN]
        lane = iota((16, GROUP), 1) % SPAN
        block = lane // 16
        parts = []
        for b in range(4):
            listed = block == facts[p, BLOCKS + 4 * b]
            for j in range(1, 4):
                listed = listed | (block == facts[p, BLOCKS + 4 * b + j])
            parts.append(jnp.where(listed & (lane <= iota((16, GROUP), 0) + 16 * b), 1.0, 0.0))
        allowed = jnp.concatenate(parts, axis=0)
        share = jnp.where(iota((SPAN, GROUP), 0) < length, 1.0, 0.0)
        scale = length.astype(F32)
        for g in range(3):
            cols = pl.ds(g * GROUP, GROUP)
            query = qkv[rows, cols]
            keys = spread_heads(qkv[rows, pl.ds(D + g * GROUP, GROUP)], diag)
            values = spread_heads(qkv[rows, pl.ds(2 * D + g * GROUP, GROUP)], diag)
            score = mm_t(query, keys) * (4.0 / HEAD)
            weight = jnp.exp(score) * allowed
            total = mm(weight.astype(BF), ones)
            prob = weight / total
            probs[p, :, cols] = prob.astype(BF)
            column = jnp.sum(prob * share, axis=0, keepdims=True) / scale
            got = mm(two_rows(column), values)
            mean_att[pl.ds(p, 1), cols] = got[0:1] + got[1:2]
        return c

    lax.fori_loop(0, OWNED, one_view, 0)
    hi, lo = split_hi_lo(mean_att[...])
    pooled[...] += mm(hi, wout[...]) + mm(lo, wout[...])


def loss_kernel(pooled, facts, d_pooled, mine, everyone, d_embed, send, recv):
    w = lax.axis_index("wide")
    z = lax.axis_index("narrow")
    barrier = pltpu.get_barrier_semaphore()
    for k in range(1, NARROW):
        pl.semaphore_signal(barrier, inc=1, device_id=(w, (z + k) % NARROW), device_id_type=MESH)
    pool = pooled[...]
    inv = lax.rsqrt(jnp.sum(pool * pool, axis=1, keepdims=True) + EPS)
    embed = pool * inv
    mine[:, 0:D] = embed
    mine[:, D : D + 128] = jnp.broadcast_to(facts[:, OFF : OFF + 1].astype(F32), (OWNED, 128))
    everyone[z] = mine[...]
    pl.semaphore_wait(barrier, NARROW - 1)
    copies = []
    for k in range(1, NARROW):
        copy = pltpu.make_async_remote_copy(
            src_ref=mine, dst_ref=everyone.at[z], send_sem=send.at[k], recv_sem=recv.at[k],
            device_id=(w, (z + k) % NARROW), device_id_type=MESH,
        )
        copy.start()
        copies.append(copy)
    for k in range(1, NARROW):
        s = (z + NARROW - k) % NARROW
        pltpu.make_async_remote_copy(
            src_ref=mine, dst_ref=everyone.at[s], send_sem=send.at[k], recv_sem=recv.at[k],
            device_id=(w, s), device_id_type=MESH,
        ).wait_recv()
    total = NARROW * OWNED
    full = everyone[...].reshape(total, D + 128)
    group = full[:, 0:D]
    offset = full[:, D : D + total].astype(I32)
    high = lax.Precision.HIGHEST
    logit = (
        lax.dot_general(
            group, group, (((1,), (1,)), ((), ())), precision=high, preferred_element_type=F32
        )
        / 0.1
    )
    row = iota((total, total), 0)
    col = iota((total, total), 1)
    positive = ((row // OWNED + offset) % NARROW) * OWNED + row % OWNED
    weight = jnp.where(row != col, jnp.exp(logit), 0.0)
    prob = weight / jnp.sum(weight, axis=1, keepdims=True)
    coef = (512.0 / 0.1) * (prob - jnp.where(col == positive, 1.0, 0.0))
    d_embed[...] = jnp.dot(
        coef, group, precision=high, preferred_element_type=F32
    ) + lax.dot_general(
        coef, group, (((0,), (0,)), ((), ())), precision=high, preferred_element_type=F32
    )
    own = d_embed[pl.ds(pl.multiple_of(OWNED * z, OWNED), OWNED), :]
    d_pooled[...] = inv * (own - embed * jnp.sum(own * embed, axis=1, keepdims=True))
    for copy in copies:
        copy.wait_send()


def backward_kernel(
    facts, d_pooled, mean_att, normed, qkv, inv_heads, inv_tokens, probs, wqkv, wout,
    d_hist, d_w, d_att, g_mixed, normed_t, d_normed,
):
    diag = head_diag()
    ones = jnp.where(diag, 1.0, 0.0).astype(BF)
    hi, lo = split_hi_lo(d_pooled[...])
    d_att[...] = mm_t(hi, wout[...]) + mm_t(lo, wout[...])
    att_hi, att_lo = split_hi_lo(mean_att[...])
    for j in range(3):
        cols = pl.ds(j * GROUP, GROUP)
        got = mm_l(
            jnp.concatenate([att_hi, att_lo], axis=0),
            jnp.concatenate([hi, hi], axis=0)[:, j * GROUP : (j + 1) * GROUP],
        )
        d_w[:, :, pl.ds(3 * D + j * GROUP, GROUP)] = got.reshape(WIDE, WROWS, GROUP).astype(BF)
    normed_t[...] = normed[...].T

    def one_view(p, c):
        rows = pl.ds(pl.multiple_of(p * SPAN, SPAN), SPAN)
        length = facts[p, LEN]
        share = jnp.where(iota((SPAN, GROUP), 0) < length, 1.0, 0.0)
        scale = length.astype(F32)
        for g in range(3):
            cols = pl.ds(g * GROUP, GROUP)
            kcols = pl.ds(D + g * GROUP, GROUP)
            vcols = pl.ds(2 * D + g * GROUP, GROUP)
            query = qkv[rows, cols]
            keys = spread_heads(qkv[rows, kcols], diag)
            values = spread_heads(qkv[rows, vcols], diag)
            d_row = d_att[pl.ds(p, 1), cols] / scale
            got = mm_t(two_rows(d_row), values)
            slope = got[0:1] + got[1:2]
            prob = probs[p, :, cols].astype(F32) * share
            tilted = prob * slope
            center = mm(tilted.astype(BF), ones)
            d_score = ((tilted - prob * center) * (4.0 / HEAD)).astype(BF)
            g_mixed[rows, cols] = mm(d_score, keys).astype(BF)
            g_mixed[rows, kcols] = gather_heads(mm_l(d_score, query), diag).astype(BF)
            d_rows = jnp.broadcast_to(d_row, (SPAN, GROUP)).astype(BF)
            g_mixed[rows, vcols] = gather_heads(mm_l(prob.astype(BF), d_rows), diag).astype(BF)
        return c

    lax.fori_loop(0, OWNED, one_view, 0)
    for j in range(6):
        cols = pl.ds(j * GROUP, GROUP)
        unit = qkv[:, cols].astype(F32)
        grad = g_mixed[:, cols].astype(F32)
        mean = mm((grad * unit).astype(BF), ones) * (1.0 / HEAD)
        g_mixed[:, cols] = (inv_heads[:, cols].astype(F32) * (grad - unit * mean)).astype(BF)
    for j in range(9):
        cols = pl.ds(j * GROUP, GROUP)
        got = mm(normed_t[...], g_mixed[:, cols])
        d_w[:, :, cols] = got.reshape(WIDE, WROWS, GROUP).astype(BF)
    for j in range(3):
        cols = pl.ds(j * GROUP, GROUP)
        d_normed[:, cols] = mm_t(g_mixed[...], wqkv[cols, :])
    for p in range(OWNED):
        rows = pl.ds(p * SPAN, SPAN)
        length = facts[p, LEN]
        start = facts[p, START]
        unit = normed[rows, :].astype(F32)
        grad = d_normed[rows, :]
        mean = jnp.sum(grad * unit, axis=1, keepdims=True) * (1.0 / D)
        back = inv_tokens[rows, 0:1] * (grad - unit * mean)
        back = back + d_pooled[p : p + 1, :] / length.astype(F32)
        alive = iota((SPAN, D), 0) < length
        d_tokens = jnp.where(alive, back, 0.0).astype(BF)
        put = jnp.where(iota((HIST, SPAN), 0) == iota((HIST, SPAN), 1) + start, 1.0, 0.0)
        spread = mm(put.astype(BF), d_tokens)
        for j in range(NARROW):
            d_hist[j, p] = spread[j * ORROWS : (j + 1) * ORROWS].astype(BF)


def return_kernel(
    place, dest, d_hist, d_w, out_hist, out_qkv, out_out,
    zin, dsum, sbuf, rbuf, core_in, acc, in_a, in_b, mid_a, mid_b, end_a, end_b,
    final, zbuf, zlast,
    zsend, zrecv, bsend, brecv, csem, asend, arecv, a2send, a2recv, lsend, lrecv,
):
    w = lax.axis_index("wide")
    z = lax.axis_index("narrow")
    core = w % 2
    x = (w // 2) % CHIP_X
    y = w // (2 * CHIP_X)
    barrier = pltpu.get_barrier_semaphore()

    def greet(k, c):
        pl.semaphore_signal(barrier, inc=1, device_id=((w + k) % WIDE, z), device_id_type=MESH)
        return c

    lax.fori_loop(1, WIDE, greet, 0)
    for k in range(1, NARROW):
        pl.semaphore_signal(barrier, inc=1, device_id=(w, (z + k) % NARROW), device_id_type=MESH)
    pl.semaphore_wait(barrier, WIDE - 1 + NARROW - 1)

    def remote(src, dst, send, recv, to):
        return pltpu.make_async_remote_copy(
            src_ref=src, dst_ref=dst, send_sem=send, recv_sem=recv, device_id=to,
            device_id_type=MESH,
        )

    other = w + 1 - 2 * core
    cross = remote(d_w.at[:, 1 - core], core_in, csem.at[0], csem.at[1], (other, z))
    cross.start()
    z_copies = []
    for k in range(1, NARROW):
        t = (z + k) % NARROW
        copy = remote(d_hist.at[t], zin.at[k], zsend.at[k], zrecv.at[k], (w, t))
        copy.start()
        z_copies.append(copy)
    cross.wait_recv()

    def pair(i, c):
        acc[i // CHIP_X, i % CHIP_X] = (
            d_w[i, core].astype(F32) + core_in[i].astype(F32)
        ).astype(BF)
        return c

    lax.fori_loop(0, CHIP_X * CHIP_Y, pair, 0)
    first = []
    for k in range(1, 4):
        tx = (x + k) % CHIP_X
        ty = (y + k) % CHIP_Y
        first.append(
            remote(
                acc.at[:, tx, :, pl.ds(0, HALF)], in_a.at[k], asend.at[0, k], arecv.at[0, k],
                ((y * CHIP_X + tx) * 2 + core, z),
            )
        )
        first.append(
            remote(
                acc.at[ty, :, :, pl.ds(HALF, HALF)], in_b.at[k], asend.at[1, k], arecv.at[1, k],
                ((ty * CHIP_X + x) * 2 + core, z),
            )
        )
    for copy in first:
        copy.start()

    for copy in z_copies:
        copy.wait_recv()

    def add_views(p, c):
        dsum[p] = (
            (d_hist[z, p].astype(F32) + zin[1, p].astype(F32))
            + (zin[2, p].astype(F32) + zin[3, p].astype(F32))
        ).astype(BF)
        return c

    lax.fori_loop(0, OWNED, add_views, 0)

    def box_copy(k):
        return remote(
            sbuf.at[k], rbuf.at[w], bsend.at[k], brecv.at[k], ((w + k) % WIDE, z)
        )

    def send_box(k, c):
        sbuf[k] = dsum[place[(w + k) % WIDE]]
        box_copy(k).start()
        return c

    lax.fori_loop(1, WIDE, send_box, 0)
    rbuf[w] = dsum[place[w]]

    for copy in first:
        copy.wait_recv()

    def middle(i, c):
        mid_a[i] = (
            (acc[i, x, :, 0:HALF].astype(F32) + in_a[1, i].astype(F32))
            + (in_a[2, i].astype(F32) + in_a[3, i].astype(F32))
        ).astype(BF)
        mid_b[i] = (
            (acc[y, i, :, HALF:WCOLS].astype(F32) + in_b[1, i].astype(F32))
            + (in_b[2, i].astype(F32) + in_b[3, i].astype(F32))
        ).astype(BF)
        return c

    lax.fori_loop(0, 4, middle, 0)
    second = []
    for k in range(1, 4):
        tx = (x + k) % CHIP_X
        ty = (y + k) % CHIP_Y
        second.append(
            remote(
                mid_a.at[ty], end_a.at[k], a2send.at[0, k], a2recv.at[0, k],
                ((ty * CHIP_X + x) * 2 + core, z),
            )
        )
        second.append(
            remote(
                mid_b.at[tx], end_b.at[k], a2send.at[1, k], a2recv.at[1, k],
                ((y * CHIP_X + tx) * 2 + core, z),
            )
        )
    for copy in second:
        copy.start()
    for copy in second:
        copy.wait_recv()
    final[0:WROWS, 0:HALF] = (mid_a[y].astype(F32) + end_a[1].astype(F32)) + (
        end_a[2].astype(F32) + end_a[3].astype(F32)
    )
    final[0:WROWS, HALF:WCOLS] = (mid_b[x].astype(F32) + end_b[1].astype(F32)) + (
        end_b[2].astype(F32) + end_b[3].astype(F32)
    )
    final[WROWS : WROWS + 8, :] = jnp.zeros((8, WCOLS), F32)
    for j in range(NARROW):
        zbuf[j] = final[6 * j : 6 * j + 8, :]
    last = []
    for k in range(1, NARROW):
        t = (z + k) % NARROW
        copy = remote(zbuf.at[t], zlast.at[k], lsend.at[k], lrecv.at[k], (w, t))
        copy.start()
        last.append(copy)

    def wait_box(k, c):
        s = (w + WIDE - k) % WIDE
        remote(sbuf.at[k], rbuf.at[s], bsend.at[k], brecv.at[k], (s, z)).wait_recv()
        return c

    lax.fori_loop(1, WIDE, wait_box, 0)

    def write(a, c):
        owner = dest[a]
        got = rbuf[jnp.maximum(owner, 0)].astype(F32)
        out_hist[a] = jnp.where(jnp.full((ORROWS, D), owner, I32) >= 0, got, 0.0)
        return c

    lax.fori_loop(0, SLOTS, write, 0)
    for copy in last:
        copy.wait_recv()
    total = (zbuf[z] + zlast[1]) + (zlast[2] + zlast[3])
    out_qkv[...] = total[0:6, 0 : 3 * D]
    out_out[...] = total[0:6, 3 * D : WCOLS]

    cross.wait_send()
    for copy in z_copies + first + second + last:
        copy.wait_send()

    def drain(k, c):
        box_copy(k).wait_send()
        return c

    lax.fori_loop(1, WIDE, drain, 0)


VM = pl.BlockSpec(memory_space=pltpu.VMEM)
SM = pl.BlockSpec(memory_space=pltpu.SMEM)
HB = pl.BlockSpec(memory_space=pl.ANY)
DMA = pltpu.SemaphoreType.DMA


def shape(dims, kind):
    return jax.ShapeDtypeStruct(dims, kind)


def remote_params(number):
    return pltpu.CompilerParams(
        collective_id=number, has_side_effects=True, vmem_limit_bytes=VMEM_LIMIT
    )


def dispatch(message, history):
    return pl.pallas_call(
        dispatch_kernel,
        out_shape=(
            shape((NARROW, OWNED, QROWS, QCOLS), BF),
            shape((OWNED, 1, 128), I32),
            shape((WIDE,), I32),
        ),
        in_specs=[SM, VM, HB],
        out_specs=(VM, VM, SM),
        scratch_shapes=[
            pltpu.VMEM((SLOTS, QROWS, QCOLS), BF),
            pltpu.VMEM((WIDE, QROWS, QCOLS), BF),
            pltpu.VMEM((WIDE, QROWS, QCOLS), BF),
            pltpu.VMEM((WIDE, 1, 128), I32),
            pltpu.SMEM((WIDE, 1, 128), I32),
            DMA, DMA,
            DMA((WIDE,)), DMA((WIDE,)), DMA((WIDE,)), DMA((WIDE,)),
            DMA((6,)), DMA((6,)),
        ],
        compiler_params=remote_params(0),
        name="dispatch",
    )(message, message.reshape(WIDE, 1, 128), history)


def forward(facts, hist, wqkv, wout):
    return pl.pallas_call(
        forward_kernel,
        out_shape=(
            shape((ROWS, D), BF),
            shape((ROWS, 3 * D), BF),
            shape((ROWS, 2 * D), BF),
            shape((ROWS, 128), F32),
            shape((OWNED, SPAN, D), BF),
            shape((OWNED, D), F32),
            shape((OWNED, D), F32),
        ),
        in_specs=[SM, VM, VM, VM],
        out_specs=(VM,) * 7,
        compiler_params=pltpu.CompilerParams(vmem_limit_bytes=VMEM_LIMIT),
        name="forward",
    )(facts, hist, wqkv, wout)


def loss_gradient(pooled, facts):
    return pl.pallas_call(
        loss_kernel,
        out_shape=shape((OWNED, D), F32),
        in_specs=[VM, VM],
        out_specs=VM,
        scratch_shapes=[
            pltpu.VMEM((OWNED, D + 128), F32),
            pltpu.VMEM((NARROW, OWNED, D + 128), F32),
            pltpu.VMEM((NARROW * OWNED, D), F32),
            DMA((NARROW,)), DMA((NARROW,)),
        ],
        compiler_params=remote_params(1),
        name="loss",
    )(pooled, facts)


def backward(facts, d_pooled, mean_att, normed, qkv, inv_heads, inv_tokens, probs, wqkv, wout):
    return pl.pallas_call(
        backward_kernel,
        out_shape=(
            shape((NARROW, OWNED, ORROWS, D), BF),
            shape((WIDE, WROWS, WCOLS), BF),
        ),
        in_specs=[SM] + [VM] * 9,
        out_specs=(VM, VM),
        scratch_shapes=[
            pltpu.VMEM((OWNED, D), F32),
            pltpu.VMEM((ROWS, 3 * D), BF),
            pltpu.VMEM((D, ROWS), BF),
            pltpu.VMEM((ROWS, D), F32),
        ],
        compiler_params=pltpu.CompilerParams(vmem_limit_bytes=VMEM_LIMIT),
        name="backward",
    )(facts, d_pooled, mean_att, normed, qkv, inv_heads, inv_tokens, probs, wqkv, wout)


def send_back(place, dest, d_hist, d_w):
    return pl.pallas_call(
        return_kernel,
        out_shape=(
            shape((SLOTS, ORROWS, D), F32),
            shape((6, 3 * D), F32),
            shape((6, D), F32),
        ),
        in_specs=[SM, SM, VM, VM],
        out_specs=(VM, VM, VM),
        scratch_shapes=[
            pltpu.VMEM((NARROW, OWNED, ORROWS, D), BF),
            pltpu.VMEM((OWNED, ORROWS, D), BF),
            pltpu.VMEM((WIDE, ORROWS, D), BF),
            pltpu.VMEM((WIDE, ORROWS, D), BF),
            pltpu.VMEM((16, WROWS, WCOLS), BF),
            pltpu.VMEM((4, 4, WROWS, WCOLS), BF),
            pltpu.VMEM((4, 4, WROWS, HALF), BF),
            pltpu.VMEM((4, 4, WROWS, HALF), BF),
            pltpu.VMEM((4, WROWS, HALF), BF),
            pltpu.VMEM((4, WROWS, HALF), BF),
            pltpu.VMEM((4, WROWS, HALF), BF),
            pltpu.VMEM((4, WROWS, HALF), BF),
            pltpu.VMEM((WROWS + 8, WCOLS), F32),
            pltpu.VMEM((NARROW, 8, WCOLS), F32),
            pltpu.VMEM((NARROW, 8, WCOLS), F32),
            DMA((NARROW,)), DMA((NARROW,)),
            DMA((WIDE,)), DMA((WIDE,)),
            DMA((2,)),
            DMA((2, 4)), DMA((2, 4)),
            DMA((2, 4)), DMA((2, 4)),
            DMA((NARROW,)), DMA((NARROW,)),
        ],
        compiler_params=remote_params(2),
        name="send_back",
    )(place, dest, d_hist, d_w.reshape(16, 2, WROWS, WCOLS))


def on_device(
    history, w_qkv, w_out, dest_owner, view_start, view_length, block_list, positive_offset
):
    order = jnp.arange(SLOTS, dtype=I32)
    facts = jnp.concatenate(
        [
            jnp.ones((SLOTS, 1), I32),
            view_length,
            positive_offset,
            view_start,
            order[:, None],
            block_list.reshape(SLOTS, 16),
            jnp.zeros((SLOTS, 128 - 21), I32),
        ],
        axis=1,
    )
    to = dest_owner[None, :] == jnp.arange(WIDE, dtype=I32)[:, None]
    message = jnp.sum(jnp.where(to[:, :, None], facts[None], 0), axis=1, dtype=I32)
    hist, facts8, place = dispatch(message, history)
    facts8 = facts8.reshape(OWNED, 128)
    normed, qkv, inv_heads, inv_tokens, probs, pooled, mean_att = forward(
        facts8, hist, w_qkv, w_out
    )
    d_pooled = loss_gradient(pooled, facts8)
    d_hist, d_w = backward(
        facts8, d_pooled, mean_att, normed, qkv, inv_heads, inv_tokens, probs, w_qkv, w_out
    )
    return send_back(place, dest_owner, d_hist, d_w)


def solution(mesh):
    return jax.shard_map(
        on_device,
        mesh=mesh,
        in_specs=(
            P("wide", None, None),
            P(),
            P(),
            P("wide"),
            P("wide", "narrow"),
            P("wide", "narrow"),
            P("wide", "narrow", None, None),
            P("wide", "narrow"),
        ),
        out_specs=(
            P("wide", "narrow", None),
            P(("wide", "narrow"), None),
            P(("wide", "narrow"), None),
        ),
        check_vma=False,
    )
```

time: 1180 us -> 152 us (0.13); the launches traced: 1160 us -> 151 us
  blocking collectives: 377 us -> 0 us
  local copies, waits for them, and re-layouts: 256 us -> 6.69 us
  starting transfers between devices: 183 us -> 0 us
  other arithmetic: 179 us -> 1.42 us
  Pallas kernels: 0 us -> 142 us
  waiting for transfers between devices: 83.5 us -> 0 us
  matrix products: 62.7 us -> 0 us
  between operations: 16.3 us -> 0.68 us
    unnamed x1 -> x0, blocking collectives: 364 us -> none
    unnamed x65 -> x0, starting transfers between devices: 160 us -> none
    pallas_call x0 -> x5, Pallas kernels: none -> 142 us  [the longest x1 54.3 us: send_back(): pl.pallas_call(return_kernel, out_shape=(shape((SLOTS, ORROWS, D), F32),...]
    scatter x33 -> x0, other arithmetic: 90.7 us -> none
    unnamed x112 -> x10, local copies, waits for them, and re-layouts: 78.2 us -> 5.83 us
    all_to_all x3 -> x0, waiting for transfers between devices: 67.8 us -> none  [the longest x1 38.1 us: on_device(): lax.all_to_all(back.reshape(wide, capacity, span, width), 'wide', split_a...]
    dot_general x15 -> x0, matrix products: 62.7 us -> none  [the longest x3 20.8 us: view_forward(): jnp.einsum('cqihd,cqjhd->cqhij', query, keys, preferred_element_type=jnp....]
    scatter x49 -> x0, local copies, waits for them, and re-layouts: 60.9 us -> none
  transfers between devices with their start and end apart: 69 -> 0, of which waited for: 3 -> 0; matrix products, arithmetic and copies ran while one was open for 42% -> 0% of each run, Pallas kernels for 0% -> 0%
where the time goes in v1:
time: 152 us; the launch traced here: 151 us
  Pallas kernels  142 us (93%)
  local copies, waits for them, and re-layouts  6.69 us (4%)
    pallas_call x1, Pallas kernels, send_back(): pl.pallas_call(return_kernel, out_shape=(shape((SLOTS, ORROWS, D), F32),...  54.3 us
    pallas_call x1, Pallas kernels, dispatch(): pl.pallas_call(dispatch_kernel, out_shape=(shape((NARROW, OWNED, QROWS, Q...  41.2 us
    pallas_call x1, Pallas kernels, backward(): pl.pallas_call(backward_kernel, out_shape=(shape((NARROW, OWNED, ORROWS,...  23.1 us
    pallas_call x1, Pallas kernels, forward(): pl.pallas_call(forward_kernel, out_shape=(shape((ROWS, D), BF), shape((RO...  15.9 us
    pallas_call x1, Pallas kernels, loss_gradient(): pl.pallas_call(loss_kernel, out_shape=shape((OWNED, D), F32), in_specs=[V...  7.98 us
    unnamed x10, local copies, waits for them, and re-layouts  5.83 us

profile of v1, /device:TPU:0, one launch (start us, length us, event | category | flops | bytes accessed | tf_op | source)
XLA Modules:
  0.0 151.2 jit_solution(387447650556606396)
XLA Ops:
  0.6 0.7 iota_compare_fusion
  1.3 0.7 copy.17
  2.0 0.7 copy.15
  2.8 0.8 copy.18
  3.5 0.7 copy.16
  4.3 0.1 concatenate.3
  4.4 0.8 select_reduce_fusion.msg_s
  5.1 41.2 %dispatch.1 = (bf16[4,8,48,384]{3,2,1,0:T(8,128)(2,1)}, s32[8,1,128]{2,1,0:T(1,128)}, s32[32]{0:T(128)}) custom-call(s32[32,128]{1,0:T(8,128)} %select_reduce_fusion.msg_s, s32[32,1,128]{2,1,0:T(1,128)} %bitcast.5, bf16[16,96,768]{2,1,0:T(8,128)(2,1)} %hist.1), custom_call_target="tpu_custom_call" | custom-call | tf_op jit(solution)/shard_map/dispatch/pallas_call | solution.py:606
  46.3 15.9 %forward.1 = (bf16[512,768]{1,0:T(8,128)(2,1)}, bf16[512,2304]{1,0:T(8,128)(2,1)}, bf16[512,1536]{1,0:T(8,128)(2,1)}, f32[512,128]{1,0:T(8,128)}, bf16[8,64,768]...) custom-call(s32[8,128]{1,0:T(8,128)} %bitcast.6, bf16[4,8,48,384]{3,2,1,0:T(8,128)(2,1)} %get-tuple-element.17.hist, ...), custom_call_target="tpu_custom_call" | custom-call | tf_op jit(solution)/shard_map/forward/pallas_call | solution.py:631
  62.2 8.0 %loss.1.d_pooled = f32[8,768]{1,0:T(8,128)} custom-call(f32[8,768]{1,0:T(8,128)} %get-tuple-element.18.pooled, s32[8,128]{1,0:T(8,128)} %bitcast.7), custom_call_target="tpu_custom_call" | custom-call | tf_op jit(solution)/shard_map/loss/pallas_call | solution.py:650
  70.2 23.1 %backward.1 = (bf16[4,8,24,768]{3,2,1,0:T(8,128)(2,1)}, bf16[32,24,3072]{2,1,0:T(8,128)(2,1)}) custom-call(s32[8,128]{1,0:T(8,128)} %bitcast.8, f32[8,768]{1,0:T(8,128)} %loss.1.d_pooled, f32[8,768]{1,0:T(8,128)} %get-tuple-element.19.mean_att, bf16[512,768]{1,0:T(8,128)(2,1)} %get-tuple-element.20.normed, bf16[512,2304]{1,0:T(8,128)(2,1)} %get-tuple-element.21.qkv, ...), custom_call_target="tpu_custom_call" | custom-call | tf_op jit(solution)/shard_map/backward/pallas_call | solution.py:667
  93.3 54.3 %send_back.1 = (f32[16,24,768]{2,1,0:T(8,128)}, f32[6,2304]{1,0:T(8,128)}, f32[6,768]{1,0:T(8,128)}) custom-call(s32[32]{0:T(128)} %get-tuple-element.15.place, s32[16]{0:T(128)} %dest.1, bf16[4,8,24,768]{3,2,1,0:T(8,128)(2,1)} %get-tuple-element.25.d_hist, bf16[16,2,24,3072]{3,2,1,0:T(8,128)(2,1)} %bitcast.4), custom_call_target="tpu_custom_call" | custom-call | tf_op jit(solution)/shard_map/send_back/pallas_call | solution.py:687
  147.5 0.0 copy-start
  147.5 0.0 copy-start.1
  147.6 2.4 %copy.22 = f32[16,24,768]{2,1,0:T(8,128)} copy(f32[16,24,768]{2,1,0:T(8,128)} %get-tuple-element.30) | data formatting | bytes 2359296
  149.9 0.0 copy-done
  150.0 0.6 copy.23
  150.6 0.0 copy-done.1
  150.6 0.6 copy.24
  (3 shorter events, 0.0 us)
Async XLA Ops:
  147.5 2.4 %copy-start = (f32[6,2304]{1,0:T(8,128)S(1)}, f32[6,2304]{1,0:T(8,128)}, u32[]{:S(2)}) copy-start(f32[6,2304]{1,0:T(8,128)} %get-tuple-element.31) | copy-start | bytes 165892
  147.5 3.0 %copy-start.1 = (f32[6,768]{1,0:T(8,128)S(1)}, f32[6,768]{1,0:T(8,128)}, u32[]{:S(2)}) copy-start(f32[6,768]{1,0:T(8,128)} %get-tuple-element.32) | copy-start | bytes 55300

commit v2 on v1

v2 whole, which is shorter than its diff:
```python
import jax
import jax.numpy as jnp
from jax import lax
from jax.experimental import pallas as pl
from jax.experimental.pallas import tpu as pltpu
from jax.sharding import PartitionSpec as P

BF = jnp.bfloat16
F32 = jnp.float32
I32 = jnp.int32
MESH = pl.DeviceIdType.MESH

WIDE = 32
NARROW = 4
CHIP_X = 4
CHIP_Y = 4
OWNED = 8
SLOTS = 16
D = 768
HEAD = 64
SPAN = 64
HIST = 96
GROUP = 256
ROWS = OWNED * SPAN
QROWS = HIST // 2
QCOLS = D // 2
ORROWS = HIST // NARROW
WROWS = D // WIDE
WCOLS = 4 * D
HALF = WCOLS // 2

LIVE, LEN, OFF, START, BLOCKS = 0, 1, 2, 3, 8
CHUNKS = 3
CROWS = QROWS // CHUNKS
PEERS = WIDE - 1
EPS = 1e-06
VMEM_LIMIT = 60 * 1024 * 1024


def mm(a, b):
    return jnp.dot(a, b, preferred_element_type=F32)


def mm_t(a, b):
    return lax.dot_general(a, b, (((1,), (1,)), ((), ())), preferred_element_type=F32)


def mm_l(a, b):
    return lax.dot_general(a, b, (((0,), (0,)), ((), ())), preferred_element_type=F32)


def split_hi_lo(x):
    hi = x.astype(BF)
    return hi, (x - hi.astype(F32)).astype(BF)


def iota(shape, dim):
    return lax.broadcasted_iota(I32, shape, dim)


def head_diag():
    shape = (GROUP, GROUP)
    return (iota(shape, 0) // HEAD) == (iota(shape, 1) // HEAD)


def spread_heads(x, diag):
    return jnp.where(diag, jnp.concatenate([x, x, x, x], axis=0), jnp.zeros((), x.dtype))


def gather_heads(full, diag):
    kept = jnp.where(diag, full, 0.0)
    return (kept[0:64] + kept[64:128]) + (kept[128:192] + kept[192:256])


def two_rows(x):
    hi = x.astype(BF).astype(F32)
    row = iota((8, GROUP), 0)
    return jnp.where(row == 0, hi, jnp.where(row == 1, x - hi, 0.0)).astype(BF)


def whole_kernel(
    dest, starts, lengths, offsets, lists, hist, wqkv_hbm, wout_hbm,
    out_hist, out_w,
    wqkv, wout, fact_t, fact, slot_s, message, frecv, fsm, pick_s, place_s, facts8,
    hbuf, sbuf, rbuf_0, rbuf_1, rbuf_2, crop,
    normed, normed_t, qkv, inv_heads, inv_tokens, probs, pooled, mean_att,
    mine, everyone, d_embed, d_pooled, d_att, g_mixed, d_normed, d_tokens,
    dw_a, dw_b, core_a, core_b, acc_a, acc_b, in_a, in_b, mid_a, mid_b, end_a, end_b,
    final, zbuf, zlast,
    d_hist, zhop, zcomb, zfin, dsum, sback, rback_0, rback_1, rback_2,
    wsem, lsem, fsem, factsem, boxsend, boxrecv, zsend, zrecv, esend, erecv,
    csend, crecv, asend, arecv, a2send, a2recv, lsend, lrecv,
    hsend, hrecv, backsend, backrecv,
):
    w = lax.axis_index("wide")
    z = lax.axis_index("narrow")
    core = w % 2
    x = (w // 2) % CHIP_X
    y = w // (2 * CHIP_X)
    right = (z + 1) % NARROW
    left = (z + 3) % NARROW
    opposite = (z + 2) % NARROW

    def remote(src, dst, send, recv, to):
        return pltpu.make_async_remote_copy(
            src_ref=src, dst_ref=dst, send_sem=send, recv_sem=recv, device_id=to,
            device_id_type=MESH,
        )

    rbuf = (rbuf_0, rbuf_1, rbuf_2)
    rback = (rback_0, rback_1, rback_2)

    load = pltpu.make_async_copy(
        hist.at[:, pl.ds(QROWS * (z // 2), QROWS), pl.ds(QCOLS * (z % 2), QCOLS)], hbuf, lsem
    )
    load.start()
    barrier = pltpu.get_barrier_semaphore()

    def greet(k, c):
        pl.semaphore_signal(barrier, inc=1, device_id=((w + k) % WIDE, z), device_id_type=MESH)
        return c

    lax.fori_loop(1, WIDE, greet, 0)
    for k in range(1, NARROW):
        pl.semaphore_signal(barrier, inc=1, device_id=(w, (z + k) % NARROW), device_id_type=MESH)
    load_qkv = pltpu.make_async_copy(wqkv_hbm, wqkv, wsem.at[0])
    load_out = pltpu.make_async_copy(wout_hbm, wout, wsem.at[1])
    load_qkv.start()
    load_out.start()

    fact_t[...] = jnp.zeros((128, 128), I32)
    fact_t[LIVE : LIVE + 1, :] = jnp.ones((1, 128), I32)
    fact_t[LEN : LEN + 1, 0:SLOTS] = lengths[...]
    fact_t[OFF : OFF + 1, 0:SLOTS] = offsets[...]
    fact_t[START : START + 1, 0:SLOTS] = starts[...]
    fact_t[BLOCKS : BLOCKS + 16, 0:SLOTS] = lists[...]
    fact[...] = fact_t[...].T
    owners = [dest[a] for a in range(SLOTS)]

    def find(d, c):
        slot = jnp.int32(0)
        live = jnp.int32(0)
        for a in range(SLOTS):
            hit = owners[a] == d
            slot = jnp.where(hit, a, slot)
            live = jnp.where(hit, 1, live)
        slot_s[d] = slot
        message[d] = fact[pl.ds(slot, 1), :] * live
        return c

    lax.fori_loop(0, WIDE, find, 0)
    pl.semaphore_wait(barrier, PEERS + NARROW - 1)

    def send_facts(k, c):
        d = (w + k) % WIDE
        remote(message.at[d], frecv.at[w], factsem.at[0], factsem.at[1], (d, z)).start()
        return c

    lax.fori_loop(1, WIDE, send_facts, 0)
    load.wait()
    for c in range(CHUNKS):

        def send_box(k, carry):
            d = (w + k) % WIDE
            sbuf[c, k] = hbuf[slot_s[d], CROWS * c : CROWS * (c + 1), :]
            remote(sbuf.at[c, k], rbuf[c].at[w], boxsend.at[c], boxrecv.at[c], (d, z)).start()
            return carry

        lax.fori_loop(1, WIDE, send_box, 0)
    frecv[w] = message[w]
    for c in range(CHUNKS):
        rbuf[c][w] = hbuf[slot_s[w], CROWS * c : CROWS * (c + 1), :]
    all_facts = remote(
        message.at[pl.ds(0, PEERS)], frecv.at[pl.ds(0, PEERS)], factsem.at[0], factsem.at[1],
        ((w + 1) % WIDE, z),
    )
    all_facts.wait_recv()
    down = pltpu.make_async_copy(frecv, fsm, fsem)
    down.start()
    down.wait()

    def scan(s, carry):
        count, picks = carry
        live = fsm[s, 0, LIVE]
        place_s[s] = jnp.minimum(count, OWNED - 1)
        picks = tuple(jnp.where((live > 0) & (count == p), s, picks[p]) for p in range(OWNED))
        return count + live, picks

    _, picks = lax.fori_loop(
        0, WIDE, scan, (jnp.int32(0), tuple(jnp.int32(0) for _ in range(OWNED)))
    )
    for p in range(OWNED):
        pick_s[p] = picks[p]
        facts8[p : p + 1, :] = frecv[picks[p]]

    def known(p, which):
        return fsm[pick_s[p], 0, which]

    part = OWNED // 2

    def hop(c, quarter, lo, size, to, n):
        where = crop.at[quarter, pl.ds(lo, size), pl.ds(CROWS * c, CROWS), :]
        return remote(where, where, zsend.at[c, n], zrecv.at[c, n], (w, to))

    z_sent = []

    def forward_hops(c):
        hop(c, left, 0, OWNED, left, 0).wait_recv()
        on_right = hop(c, left, 0, part, right, 2)
        on_right.start()
        hop(c, right, 0, OWNED, right, 1).wait_recv()
        on_left = hop(c, right, part, part, left, 3)
        on_left.start()
        z_sent.extend([on_right, on_left])

    all_boxes = []
    for c in range(CHUNKS):
        boxes = remote(
            sbuf.at[c, pl.ds(0, PEERS)], rbuf[c].at[pl.ds(0, PEERS)], boxsend.at[c],
            boxrecv.at[c], ((w + 1) % WIDE, z),
        )
        all_boxes.append(boxes)
        boxes.wait_recv()
        for p in range(OWNED):
            crop[z, p, CROWS * c : CROWS * (c + 1), :] = rbuf[c][picks[p]]
        to_right = hop(c, z, 0, OWNED, right, 0)
        to_left = hop(c, z, 0, OWNED, left, 1)
        to_right.start()
        to_left.start()
        z_sent.extend([to_right, to_left])
        if c > 0:
            forward_hops(c - 1)
    forward_hops(CHUNKS - 1)
    for c in range(CHUNKS):
        hop(c, opposite, 0, part, left, 2).wait_recv()
        hop(c, opposite, part, part, right, 3).wait_recv()

    diag = head_diag()
    ones = jnp.where(diag, 1.0, 0.0).astype(BF)
    row48 = iota((SPAN, QROWS), 0)
    col48 = iota((SPAN, QROWS), 1)
    for p in range(OWNED):
        start = known(p, START)
        length = known(p, LEN)
        rows = pl.ds(p * SPAN, SPAN)
        source = row48 + start
        alive = row48 < length
        top = jnp.where((col48 == source) & alive, 1.0, 0.0).astype(BF)
        low = jnp.where((col48 + QROWS == source) & alive, 1.0, 0.0).astype(BF)
        lhs = mm(top, crop[0, p]) + mm(low, crop[2, p])
        rhs = mm(top, crop[1, p]) + mm(low, crop[3, p])
        square = jnp.sum(lhs * lhs, axis=1, keepdims=True) + jnp.sum(
            rhs * rhs, axis=1, keepdims=True
        )
        inv = lax.rsqrt(square * (1.0 / D) + EPS)
        normed[rows, 0:QCOLS] = (lhs * inv).astype(BF)
        normed[rows, QCOLS:D] = (rhs * inv).astype(BF)
        inv_tokens[rows, :] = jnp.broadcast_to(inv, (SPAN, 128))
        scale = length.astype(F32)
        pooled[p : p + 1, 0:QCOLS] = jnp.sum(lhs, axis=0, keepdims=True) / scale
        pooled[p : p + 1, QCOLS:D] = jnp.sum(rhs, axis=0, keepdims=True) / scale
    load_qkv.wait()
    load_out.wait()
    for j in range(9):
        cols = pl.ds(j * GROUP, GROUP)
        mixed = mm(normed[...], wqkv[:, cols])
        if j < 6:
            square = mm((mixed * mixed).astype(BF), ones)
            inv = lax.rsqrt(square * (1.0 / HEAD) + EPS)
            qkv[:, cols] = (mixed * inv).astype(BF)
            inv_heads[:, cols] = inv.astype(BF)
        else:
            qkv[:, cols] = mixed.astype(BF)

    def attend(p, carry):
        rows = pl.ds(pl.multiple_of(p * SPAN, SPAN), SPAN)
        length = known(p, LEN)
        lane = iota((16, GROUP), 1) % SPAN
        block = lane // 16
        parts = []
        for b in range(4):
            listed = block == known(p, BLOCKS + 4 * b)
            for j in range(1, 4):
                listed = listed | (block == known(p, BLOCKS + 4 * b + j))
            parts.append(jnp.where(listed & (lane <= iota((16, GROUP), 0) + 16 * b), 1.0, 0.0))
        allowed = jnp.concatenate(parts, axis=0)
        share = jnp.where(iota((SPAN, GROUP), 0) < length, 1.0, 0.0)
        scale = length.astype(F32)
        for g in range(3):
            cols = pl.ds(g * GROUP, GROUP)
            query = qkv[rows, cols]
            keys = spread_heads(qkv[rows, pl.ds(D + g * GROUP, GROUP)], diag)
            values = spread_heads(qkv[rows, pl.ds(2 * D + g * GROUP, GROUP)], diag)
            score = mm_t(query, keys) * (4.0 / HEAD)
            weight = jnp.exp(score) * allowed
            total = mm(weight.astype(BF), ones)
            prob = weight / total
            probs[p, :, cols] = prob.astype(BF)
            column = jnp.sum(prob * share, axis=0, keepdims=True) / scale
            got = mm(two_rows(column), values)
            mean_att[pl.ds(p, 1), cols] = got[0:1] + got[1:2]
        return carry

    lax.fori_loop(0, OWNED, attend, 0)
    att_hi, att_lo = split_hi_lo(mean_att[...])
    pooled[...] += mm(att_hi, wout[...]) + mm(att_lo, wout[...])

    pool = pooled[...]
    inv_pool = lax.rsqrt(jnp.sum(pool * pool, axis=1, keepdims=True) + EPS)
    embed = pool * inv_pool
    mine[:, 0:D] = embed
    mine[:, D : D + 128] = jnp.broadcast_to(facts8[:, OFF : OFF + 1].astype(F32), (OWNED, 128))
    e_copies = []
    for k in range(1, NARROW):
        copy = remote(
            mine, everyone.at[z], esend.at[k], erecv.at[k], (w, (z + k) % NARROW)
        )
        copy.start()
        e_copies.append(copy)
    everyone[z] = mine[...]
    normed_t[...] = normed[...].T
    for k in range(1, NARROW):
        s = (z + NARROW - k) % NARROW
        remote(mine, everyone.at[s], esend.at[k], erecv.at[k], (w, s)).wait_recv()
    total = NARROW * OWNED
    full = everyone[...].reshape(total, D + 128)
    group = full[:, 0:D]
    offset = full[:, D : D + total].astype(I32)
    high = lax.Precision.HIGHEST
    logit = (
        lax.dot_general(
            group, group, (((1,), (1,)), ((), ())), precision=high, preferred_element_type=F32
        )
        / 0.1
    )
    row = iota((total, total), 0)
    col = iota((total, total), 1)
    positive = ((row // OWNED + offset) % NARROW) * OWNED + row % OWNED
    weight = jnp.where(row != col, jnp.exp(logit), 0.0)
    prob = weight / jnp.sum(weight, axis=1, keepdims=True)
    coef = (512.0 / 0.1) * (prob - jnp.where(col == positive, 1.0, 0.0))
    d_embed[...] = jnp.dot(
        coef, group, precision=high, preferred_element_type=F32
    ) + lax.dot_general(
        coef, group, (((0,), (0,)), ((), ())), precision=high, preferred_element_type=F32
    )
    own = d_embed[pl.ds(pl.multiple_of(OWNED * z, OWNED), OWNED), :]
    d_pooled[...] = inv_pool * (own - embed * jnp.sum(own * embed, axis=1, keepdims=True))

    hi, lo = split_hi_lo(d_pooled[...])
    d_att[...] = mm_t(hi, wout[...]) + mm_t(lo, wout[...])
    for j in range(3):
        got = mm_l(
            jnp.concatenate([att_hi, att_lo], axis=0),
            jnp.concatenate([hi, hi], axis=0)[:, j * GROUP : (j + 1) * GROUP],
        )
        dw_b[:, :, :, pl.ds(D + j * GROUP, GROUP)] = got.reshape(16, 2, WROWS, GROUP).astype(BF)

    def attend_back(p, carry):
        rows = pl.ds(pl.multiple_of(p * SPAN, SPAN), SPAN)
        length = known(p, LEN)
        share = jnp.where(iota((SPAN, GROUP), 0) < length, 1.0, 0.0)
        scale = length.astype(F32)
        for g in range(3):
            cols = pl.ds(g * GROUP, GROUP)
            kcols = pl.ds(D + g * GROUP, GROUP)
            vcols = pl.ds(2 * D + g * GROUP, GROUP)
            query = qkv[rows, cols]
            keys = spread_heads(qkv[rows, kcols], diag)
            values = spread_heads(qkv[rows, vcols], diag)
            d_row = d_att[pl.ds(p, 1), cols] / scale
            got = mm_t(two_rows(d_row), values)
            slope = got[0:1] + got[1:2]
            prob = probs[p, :, cols].astype(F32) * share
            tilted = prob * slope
            center = mm(tilted.astype(BF), ones)
            d_score = ((tilted - prob * center) * (4.0 / HEAD)).astype(BF)
            g_mixed[rows, cols] = mm(d_score, keys).astype(BF)
            g_mixed[rows, kcols] = gather_heads(mm_l(d_score, query), diag).astype(BF)
            d_rows = jnp.broadcast_to(d_row, (SPAN, GROUP)).astype(BF)
            g_mixed[rows, vcols] = gather_heads(mm_l(prob.astype(BF), d_rows), diag).astype(BF)
        return carry

    lax.fori_loop(0, OWNED, attend_back, 0)
    for j in range(3):
        got = mm(normed_t[...], g_mixed[:, pl.ds(2 * D + j * GROUP, GROUP)])
        dw_b[:, :, :, pl.ds(j * GROUP, GROUP)] = got.reshape(16, 2, WROWS, GROUP).astype(BF)
    other = w + 1 - 2 * core
    cross_b = remote(dw_b.at[:, 1 - core], core_b, csend.at[1], crecv.at[1], (other, z))
    cross_b.start()
    for j in range(6):
        cols = pl.ds(j * GROUP, GROUP)
        unit = qkv[:, cols].astype(F32)
        grad = g_mixed[:, cols].astype(F32)
        mean = mm((grad * unit).astype(BF), ones) * (1.0 / HEAD)
        back = (inv_heads[:, cols].astype(F32) * (grad - unit * mean)).astype(BF)
        g_mixed[:, cols] = back
        got = mm(normed_t[...], back)
        dw_a[:, :, :, cols] = got.reshape(16, 2, WROWS, GROUP).astype(BF)
    cross_a = remote(dw_a.at[:, 1 - core], core_a, csend.at[0], crecv.at[0], (other, z))
    cross_a.start()
    cross_b.wait_recv()

    def pair_b(i, carry):
        acc_b[i // CHIP_X, i % CHIP_X] = (
            dw_b[i, core].astype(F32) + core_b[i].astype(F32)
        ).astype(BF)
        return carry

    lax.fori_loop(0, CHIP_X * CHIP_Y, pair_b, 0)
    first = []
    for k in range(1, 4):
        ty = (y + k) % CHIP_Y
        first.append(
            remote(
                acc_b.at[ty], in_b.at[k], asend.at[1, k], arecv.at[1, k],
                ((ty * CHIP_X + x) * 2 + core, z),
            )
        )
        first[-1].start()
    for j in range(3):
        cols = pl.ds(j * GROUP, GROUP)
        d_normed[:, cols] = mm_t(g_mixed[...], wqkv[cols, :])
    cross_a.wait_recv()

    def pair_a(i, carry):
        acc_a[i % CHIP_X, i // CHIP_X] = (
            dw_a[i, core].astype(F32) + core_a[i].astype(F32)
        ).astype(BF)
        return carry

    lax.fori_loop(0, CHIP_X * CHIP_Y, pair_a, 0)
    for k in range(1, 4):
        tx = (x + k) % CHIP_X
        first.append(
            remote(
                acc_a.at[tx], in_a.at[k], asend.at[0, k], arecv.at[0, k],
                ((y * CHIP_X + tx) * 2 + core, z),
            )
        )
        first[-1].start()
    for p in range(OWNED):
        rows = pl.ds(p * SPAN, SPAN)
        length = known(p, LEN)
        unit = normed[rows, :].astype(F32)
        grad = d_normed[rows, :]
        mean = jnp.sum(grad * unit, axis=1, keepdims=True) * (1.0 / D)
        back = inv_tokens[rows, 0:1] * (grad - unit * mean)
        back = back + d_pooled[p : p + 1, :] / length.astype(F32)
        alive = iota((SPAN, D), 0) < length
        d_tokens[rows, :] = jnp.where(alive, back, 0.0).astype(BF)

    h_sent = []
    shift = iota((HIST, SPAN), 0) - iota((HIST, SPAN), 1)

    def hpiece(c, quarter, lo):
        return d_hist.at[c, quarter, pl.ds(lo, part)]

    for c in range(CHUNKS):
        for p in range(OWNED):
            put = jnp.where(shift == known(p, START), 1.0, 0.0).astype(BF)
            spread = mm(put, d_tokens[p * SPAN : (p + 1) * SPAN, c * GROUP : (c + 1) * GROUP])
            for j in range(NARROW):
                d_hist[c, j, p] = spread[j * ORROWS : (j + 1) * ORROWS].astype(BF)
        for copy in (
            remote(hpiece(c, opposite, 0), zhop.at[c, 0], hsend.at[c, 0], hrecv.at[c, 0], (w, right)),
            remote(hpiece(c, opposite, part), zhop.at[c, 1], hsend.at[c, 1], hrecv.at[c, 1], (w, left)),
            remote(hpiece(c, right, part), zfin.at[c, 1], hsend.at[c, 2], hrecv.at[c, 2], (w, right)),
            remote(hpiece(c, left, 0), zfin.at[c, 2], hsend.at[c, 3], hrecv.at[c, 3], (w, left)),
        ):
            copy.start()
            h_sent.append(copy)
    for c in range(CHUNKS):
        remote(hpiece(c, opposite, 0), zhop.at[c, 0], hsend.at[c, 0], hrecv.at[c, 0], (w, left)).wait_recv()
        for p in range(part):
            zcomb[c, 0, p] = (
                d_hist[c, right, p].astype(F32) + zhop[c, 0, p].astype(F32)
            ).astype(BF)
        on_right = remote(
            zcomb.at[c, 0], zfin.at[c, 0], hsend.at[c, 4], hrecv.at[c, 4], (w, right)
        )
        on_right.start()
        remote(hpiece(c, opposite, part), zhop.at[c, 1], hsend.at[c, 1], hrecv.at[c, 1], (w, right)).wait_recv()
        for p in range(part):
            zcomb[c, 1, p] = (
                d_hist[c, left, part + p].astype(F32) + zhop[c, 1, p].astype(F32)
            ).astype(BF)
        on_left = remote(
            zcomb.at[c, 1], zfin.at[c, 3], hsend.at[c, 5], hrecv.at[c, 5], (w, left)
        )
        on_left.start()
        h_sent.extend([on_right, on_left])
    all_back = []
    for c in range(CHUNKS):
        remote(zcomb.at[c, 0], zfin.at[c, 0], hsend.at[c, 4], hrecv.at[c, 4], (w, left)).wait_recv()
        remote(hpiece(c, right, part), zfin.at[c, 1], hsend.at[c, 2], hrecv.at[c, 2], (w, left)).wait_recv()
        remote(hpiece(c, left, 0), zfin.at[c, 2], hsend.at[c, 3], hrecv.at[c, 3], (w, right)).wait_recv()
        remote(zcomb.at[c, 1], zfin.at[c, 3], hsend.at[c, 5], hrecv.at[c, 5], (w, right)).wait_recv()
        for p in range(part):
            dsum[c, p] = (
                (d_hist[c, z, p].astype(F32) + zfin[c, 0, p].astype(F32))
                + zfin[c, 2, p].astype(F32)
            ).astype(BF)
            dsum[c, part + p] = (
                (d_hist[c, z, part + p].astype(F32) + zfin[c, 1, p].astype(F32))
                + zfin[c, 3, p].astype(F32)
            ).astype(BF)

        def send_back(k, carry):
            d = (w + k) % WIDE
            sback[c, k] = dsum[c, place_s[d]]
            remote(sback.at[c, k], rback[c].at[w], backsend.at[c], backrecv.at[c], (d, z)).start()
            return carry

        lax.fori_loop(1, WIDE, send_back, 0)
        rback[c][w] = dsum[c, place_s[w]]
        all_back.append(
            remote(
                sback.at[c, pl.ds(0, PEERS)], rback[c].at[pl.ds(0, PEERS)], backsend.at[c],
                backrecv.at[c], ((w + 1) % WIDE, z),
            )
        )

    for copy in first:
        copy.wait_recv()

    def middle(i, carry):
        mid_a[i] = (
            (acc_a[x, i].astype(F32) + in_a[1, i].astype(F32))
            + (in_a[2, i].astype(F32) + in_a[3, i].astype(F32))
        ).astype(BF)
        mid_b[i] = (
            (acc_b[y, i].astype(F32) + in_b[1, i].astype(F32))
            + (in_b[2, i].astype(F32) + in_b[3, i].astype(F32))
        ).astype(BF)
        return carry

    lax.fori_loop(0, 4, middle, 0)
    second = []
    for k in range(1, 4):
        tx = (x + k) % CHIP_X
        ty = (y + k) % CHIP_Y
        second.append(
            remote(
                mid_a.at[ty], end_a.at[k], a2send.at[0, k], a2recv.at[0, k],
                ((ty * CHIP_X + x) * 2 + core, z),
            )
        )
        second.append(
            remote(
                mid_b.at[tx], end_b.at[k], a2send.at[1, k], a2recv.at[1, k],
                ((y * CHIP_X + tx) * 2 + core, z),
            )
        )
    for copy in second:
        copy.start()
    for copy in second:
        copy.wait_recv()
    final[0:WROWS, 0:HALF] = (mid_a[y].astype(F32) + end_a[1].astype(F32)) + (
        end_a[2].astype(F32) + end_a[3].astype(F32)
    )
    final[0:WROWS, HALF:WCOLS] = (mid_b[x].astype(F32) + end_b[1].astype(F32)) + (
        end_b[2].astype(F32) + end_b[3].astype(F32)
    )
    final[WROWS : WROWS + 8, :] = jnp.zeros((8, WCOLS), F32)
    for j in range(NARROW):
        zbuf[j] = final[6 * j : 6 * j + 8, :]
    last = []
    for k in range(1, NARROW):
        t = (z + k) % NARROW
        copy = remote(zbuf.at[t], zlast.at[k], lsend.at[k], lrecv.at[k], (w, t))
        copy.start()
        last.append(copy)
    for c in range(CHUNKS):
        all_back[c].wait_recv()

        def write(a, carry):
            owner = dest[a]
            got = rback[c][jnp.maximum(owner, 0)].astype(F32)
            kept = jnp.where(jnp.full((ORROWS, GROUP), owner, I32) >= 0, got, 0.0)
            out_hist[a, :, c * GROUP : (c + 1) * GROUP] = kept.astype(BF)
            return carry

        lax.fori_loop(0, SLOTS, write, 0)
    for copy in last:
        copy.wait_recv()
    out_w[...] = (zbuf[z] + zlast[1]) + (zlast[2] + zlast[3])

    all_facts.wait_send()
    cross_a.wait_send()
    cross_b.wait_send()
    for copy in all_boxes + z_sent + e_copies + first + second + last + h_sent + all_back:
        copy.wait_send()


VM = pl.BlockSpec(memory_space=pltpu.VMEM)
SM = pl.BlockSpec(memory_space=pltpu.SMEM)
HB = pl.BlockSpec(memory_space=pl.ANY)
DMA = pltpu.SemaphoreType.DMA


def vmem(kind, *dims):
    return pltpu.VMEM(dims, kind)


def on_device(
    history, w_qkv, w_out, dest_owner, view_start, view_length, block_list, positive_offset
):
    d_history, d_w = pl.pallas_call(
        whole_kernel,
        out_shape=(
            jax.ShapeDtypeStruct((SLOTS, ORROWS, D), BF),
            jax.ShapeDtypeStruct((8, WCOLS), F32),
        ),
        in_specs=[SM, VM, VM, VM, VM, HB, HB, HB],
        out_specs=(VM, VM),
        scratch_shapes=[
            vmem(BF, D, 3 * D),
            vmem(BF, D, D),
            vmem(I32, 128, 128),
            vmem(I32, 128, 128),
            pltpu.SMEM((WIDE,), I32),
            vmem(I32, WIDE, 1, 128),
            vmem(I32, WIDE, 1, 128),
            pltpu.SMEM((WIDE, 1, 128), I32),
            pltpu.SMEM((OWNED,), I32),
            pltpu.SMEM((WIDE,), I32),
            vmem(I32, OWNED, 128),
            vmem(BF, SLOTS, QROWS, QCOLS),
            vmem(BF, CHUNKS, WIDE, CROWS, QCOLS),
            vmem(BF, WIDE, CROWS, QCOLS),
            vmem(BF, WIDE, CROWS, QCOLS),
            vmem(BF, WIDE, CROWS, QCOLS),
            vmem(BF, NARROW, OWNED, QROWS, QCOLS),
            vmem(BF, ROWS, D),
            vmem(BF, D, ROWS),
            vmem(BF, ROWS, 3 * D),
            vmem(BF, ROWS, 2 * D),
            vmem(F32, ROWS, 128),
            vmem(BF, OWNED, SPAN, D),
            vmem(F32, OWNED, D),
            vmem(F32, OWNED, D),
            vmem(F32, OWNED, D + 128),
            vmem(F32, NARROW, OWNED, D + 128),
            vmem(F32, NARROW * OWNED, D),
            vmem(F32, OWNED, D),
            vmem(F32, OWNED, D),
            vmem(BF, ROWS, 3 * D),
            vmem(F32, ROWS, D),
            vmem(BF, ROWS, D),
            vmem(BF, 16, 2, WROWS, HALF),
            vmem(BF, 16, 2, WROWS, HALF),
            vmem(BF, 16, WROWS, HALF),
            vmem(BF, 16, WROWS, HALF),
            vmem(BF, 4, 4, WROWS, HALF),
            vmem(BF, 4, 4, WROWS, HALF),
            vmem(BF, 4, 4, WROWS, HALF),
            vmem(BF, 4, 4, WROWS, HALF),
            vmem(BF, 4, WROWS, HALF),
            vmem(BF, 4, WROWS, HALF),
            vmem(BF, 4, WROWS, HALF),
            vmem(BF, 4, WROWS, HALF),
            vmem(F32, WROWS + 8, WCOLS),
            vmem(F32, NARROW, 8, WCOLS),
            vmem(F32, NARROW, 8, WCOLS),
            vmem(BF, CHUNKS, NARROW, OWNED, ORROWS, GROUP),
            vmem(BF, CHUNKS, 2, OWNED // 2, ORROWS, GROUP),
            vmem(BF, CHUNKS, 2, OWNED // 2, ORROWS, GROUP),
            vmem(BF, CHUNKS, 4, OWNED // 2, ORROWS, GROUP),
            vmem(BF, CHUNKS, OWNED, ORROWS, GROUP),
            vmem(BF, CHUNKS, WIDE, ORROWS, GROUP),
            vmem(BF, WIDE, ORROWS, GROUP),
            vmem(BF, WIDE, ORROWS, GROUP),
            vmem(BF, WIDE, ORROWS, GROUP),
            DMA((2,)), DMA, DMA, DMA((2,)),
            DMA((CHUNKS,)), DMA((CHUNKS,)),
            DMA((CHUNKS, 4)), DMA((CHUNKS, 4)),
            DMA((NARROW,)), DMA((NARROW,)),
            DMA((2,)), DMA((2,)),
            DMA((2, 4)), DMA((2, 4)),
            DMA((2, 4)), DMA((2, 4)),
            DMA((NARROW,)), DMA((NARROW,)),
            DMA((CHUNKS, 6)), DMA((CHUNKS, 6)),
            DMA((CHUNKS,)), DMA((CHUNKS,)),
        ],
        compiler_params=pltpu.CompilerParams(
            collective_id=0, has_side_effects=True, vmem_limit_bytes=VMEM_LIMIT
        ),
        name="step",
    )(
        dest_owner, view_start.T, view_length.T, positive_offset.T,
        block_list.reshape(SLOTS, 16).T, history, w_qkv, w_out,
    )
    return d_history.astype(F32), d_w[0:6, 0 : 3 * D], d_w[0:6, 3 * D : WCOLS]


def solution(mesh):
    return jax.shard_map(
        on_device,
        mesh=mesh,
        in_specs=(
            P("wide", None, None),
            P(),
            P(),
            P("wide"),
            P("wide", "narrow"),
            P("wide", "narrow"),
            P("wide", "narrow", None, None),
            P("wide", "narrow"),
        ),
        out_specs=(
            P("wide", "narrow", None),
            P(("wide", "narrow"), None),
            P(("wide", "narrow"), None),
        ),
        check_vma=False,
    )
```

time: 152 us -> 116 us (0.76)
  Pallas kernels: 142 us -> 109 us
  local copies, waits for them, and re-layouts: 6.69 us -> 2.87 us
    pallas_call x5 -> x1, Pallas kernels: 142 us -> 109 us  [on_device(): pl.pallas_call(whole_kernel, out_shape=(jax.ShapeDtypeStruct((SLOTS, ORRO...]
    unnamed x10 -> x0, local copies, waits for them, and re-layouts: 5.83 us -> none
    slice x0 -> x2, local copies, waits for them, and re-layouts: none -> 2.87 us  [on_device(): return (d_history.astype(F32), d_w[0:6, 0:3 * D], d_w[0:6, 3 * D:WCOLS])]
    convert_element_type x0 -> x1, other arithmetic: none -> 2.15 us  [on_device(): return (d_history.astype(F32), d_w[0:6, 0:3 * D], d_w[0:6, 3 * D:WCOLS])]
where the time goes in v2:
time: 116 us; the launch traced here: 115 us
  Pallas kernels  109 us (94%)
  local copies, waits for them, and re-layouts  2.87 us (2%)
  other arithmetic  2.15 us (2%)
    pallas_call x1, Pallas kernels, on_device(): pl.pallas_call(whole_kernel, out_shape=(jax.ShapeDtypeStruct((SLOTS, ORRO...  109 us
    slice x2, local copies, waits for them, and re-layouts, on_device(): return (d_history.astype(F32), d_w[0:6, 0:3 * D], d_w[0:6, 3 * D:WCOLS])  2.87 us

profile of v2, /device:TPU:0, one launch (start us, length us, event | category | flops | bytes accessed | tf_op | source)
XLA Modules:
  0.0 115.2 jit_solution(9868996088265662186)
XLA Ops:
  0.6 109.5 %step.1 = (bf16[16,24,768]{2,1,0:T(8,128)(2,1)}, f32[8,3072]{1,0:T(8,128)}) custom-call(s32[16]{0:T(128)} %dest.1, s32[1,16]{1,0:T(1,128)} %bitcast.7, s32[1,16]{1,0:T(1,128)} %bitcast.8, s32[1,16]{1,0:T(1,128)} %bitcast.9, s32[16,16]{1,0:T(8,128)} %bitcast.6, bf16[16,96,768]{2,1,0:T(8,128)(2,1)} %hist.1, bf16[768,2304]{1,0:T(8,128)(2,1)} %wqkv_hbm.1, ...), custom_call_target="tpu_custom_call" | custom-call | tf_op jit(solution)/shard_map/step/pallas_call | solution.py:609
  110.1 1.3 %slice.7 = f32[6,768]{1,0:T(8,128)} slice(f32[8,3072]{1,0:T(8,128)} %get-tuple-element.6), slice={[0:6], [2304:3072]} | slice | bytes 36864 | tf_op jit(solution)/shard_map/slice | solution.py:694
  111.5 1.5 %slice.6 = f32[6,2304]{1,0:T(8,128)} slice(f32[8,3072]{1,0:T(8,128)} %get-tuple-element.6), slice={[0:6], [0:2304]} | slice | bytes 110592 | tf_op jit(solution)/shard_map/slice | solution.py:694
  113.0 2.2 %convert_element_type.3 = f32[16,24,768]{2,1,0:T(8,128)} convert(bf16[16,24,768]{2,1,0:T(8,128)(2,1)} %get-tuple-element.5) | non-fusion elementwise | flops 294912 | bytes 1769472 | tf_op jit(solution)/shard_map/convert_element_type | solution.py:694

commit v3 on v2

v3 whole, which is shorter than its diff:
```python
import jax
import jax.numpy as jnp
from jax import lax
from jax.experimental import pallas as pl
from jax.experimental.pallas import tpu as pltpu
from jax.sharding import PartitionSpec as P

BF = jnp.bfloat16
F32 = jnp.float32
I32 = jnp.int32
MESH = pl.DeviceIdType.MESH

WIDE = 32
NARROW = 4
CHIP_X = 4
CHIP_Y = 4
OWNED = 8
SLOTS = 16
D = 768
HEAD = 64
SPAN = 64
HIST = 96
GROUP = 256
ROWS = OWNED * SPAN
QROWS = HIST // 2
QCOLS = D // 2
ORROWS = HIST // NARROW
WROWS = D // WIDE
WCOLS = 4 * D

LIVE, LEN, OFF, START, BLOCKS = 0, 1, 2, 3, 8
BOXES = ((0, 16, 0, 384), (16, 16, 0, 384), (32, 16, 0, 256), (32, 16, 256, 128))
NBOX = len(BOXES)
BACKS = ((0, 128), (128, 256), (384, 256), (640, 128))
NBACK = len(BACKS)
PAIR = 2
PEERS = WIDE - 1
EPS = 1e-06
VMEM_LIMIT = 60 * 1024 * 1024


def mm(a, b):
    return jnp.dot(a, b, preferred_element_type=F32)


def mm_t(a, b):
    return lax.dot_general(a, b, (((1,), (1,)), ((), ())), preferred_element_type=F32)


def mm_l(a, b):
    return lax.dot_general(a, b, (((0,), (0,)), ((), ())), preferred_element_type=F32)


def split_hi_lo(x):
    hi = x.astype(BF)
    return hi, (x - hi.astype(F32)).astype(BF)


def iota(shape, dim):
    return lax.broadcasted_iota(I32, shape, dim)


def head_diag():
    shape = (GROUP, GROUP)
    return (iota(shape, 0) // HEAD) == (iota(shape, 1) // HEAD)


def spread_heads(x, diag):
    return jnp.where(diag, jnp.concatenate([x, x, x, x], axis=0), jnp.zeros((), x.dtype))


def gather_heads(full, diag):
    kept = jnp.where(diag, full, 0.0)
    return (kept[0:64] + kept[64:128]) + (kept[128:192] + kept[192:256])


def whole_kernel(
    dest, starts, lengths, offsets, lists, hist, wqkv_hbm, wout_hbm,
    out_hist, out_w,
    wqkv, wout, fact_t, fact, slot_s, message, frecv, fsm, pick_s, place_s, facts8,
    hbuf, crop,
    normed, normed_t, qkv, inv_heads, inv_tokens, probs, col_w, pooled, mean_att,
    mine, everyone, d_embed, d_pooled, d_att, g_mixed, d_normed, d_tokens,
    dw, core_in, acc, ring, mid, ends, final, zbuf, zlast,
    sbuf_0, sbuf_1, sbuf_2, sbuf_3, rbuf_0, rbuf_1, rbuf_2, rbuf_3,
    hist_0, hist_1, hist_2, hist_3, zin_0, zin_1, zin_2, zin_3,
    dsum_0, dsum_1, dsum_2, dsum_3, sback_0, sback_1, sback_2, sback_3,
    rback_0, rback_1, rback_2, rback_3,
    wsem, lsem, fsem, factsem, boxsend, boxrecv, zsend, zrecv, esend, erecv,
    csend, crecv, asend, arecv, a2send, a2recv, lsend, lrecv,
    hsend, hrecv, backsend, backrecv,
):
    w = lax.axis_index("wide")
    z = lax.axis_index("narrow")
    core = w % 2
    x = (w // 2) % CHIP_X
    y = w // (2 * CHIP_X)
    def remote(src, dst, send, recv, to):
        return pltpu.make_async_remote_copy(
            src_ref=src, dst_ref=dst, send_sem=send, recv_sem=recv, device_id=to,
            device_id_type=MESH,
        )

    sbuf = (sbuf_0, sbuf_1, sbuf_2, sbuf_3)
    rbuf = (rbuf_0, rbuf_1, rbuf_2, rbuf_3)
    d_hist = (hist_0, hist_1, hist_2, hist_3)
    zin = (zin_0, zin_1, zin_2, zin_3)
    dsum = (dsum_0, dsum_1, dsum_2, dsum_3)
    sback = (sback_0, sback_1, sback_2, sback_3)
    rback = (rback_0, rback_1, rback_2, rback_3)

    load = pltpu.make_async_copy(
        hist.at[:, pl.ds(QROWS * (z // 2), QROWS), pl.ds(QCOLS * (z % 2), QCOLS)], hbuf, lsem
    )
    load.start()
    barrier = pltpu.get_barrier_semaphore()

    def greet(k, c):
        pl.semaphore_signal(barrier, inc=1, device_id=((w + k) % WIDE, z), device_id_type=MESH)
        return c

    lax.fori_loop(1, WIDE, greet, 0)
    for k in range(1, NARROW):
        pl.semaphore_signal(barrier, inc=1, device_id=(w, (z + k) % NARROW), device_id_type=MESH)
    load_qkv = pltpu.make_async_copy(wqkv_hbm, wqkv, wsem.at[0])
    load_out = pltpu.make_async_copy(wout_hbm, wout, wsem.at[1])
    load_qkv.start()
    load_out.start()

    fact_t[...] = jnp.zeros((128, 128), I32)
    fact_t[LIVE : LIVE + 1, :] = jnp.ones((1, 128), I32)
    fact_t[LEN : LEN + 1, 0:SLOTS] = lengths[...]
    fact_t[OFF : OFF + 1, 0:SLOTS] = offsets[...]
    fact_t[START : START + 1, 0:SLOTS] = starts[...]
    fact_t[BLOCKS : BLOCKS + 16, 0:SLOTS] = lists[...]
    fact[...] = fact_t[...].T
    owners = [dest[a] for a in range(SLOTS)]

    def find(d, c):
        slot = jnp.int32(0)
        live = jnp.int32(0)
        for a in range(SLOTS):
            hit = owners[a] == d
            slot = jnp.where(hit, a, slot)
            live = jnp.where(hit, 1, live)
        slot_s[d] = slot
        message[d] = fact[pl.ds(slot, 1), :] * live
        return c

    lax.fori_loop(0, WIDE, find, 0)
    load.wait()

    def fill(k, carry):
        slot = slot_s[(w + k) % WIDE]
        for c, (r0, nr, c0, nc) in enumerate(BOXES):
            sbuf[c][k] = hbuf[slot, r0 : r0 + nr, c0 : c0 + nc]
        return carry

    lax.fori_loop(1, WIDE, fill, 0)
    frecv[w] = message[w]
    for c, (r0, nr, c0, nc) in enumerate(BOXES):
        rbuf[c][w] = hbuf[slot_s[w], r0 : r0 + nr, c0 : c0 + nc]
    pl.semaphore_wait(barrier, PEERS + NARROW - 1)

    def send_facts(k, c):
        d = (w + k) % WIDE
        remote(message.at[d], frecv.at[w], factsem.at[0], factsem.at[1], (d, z)).start()
        return c

    lax.fori_loop(1, WIDE, send_facts, 0)
    for c in range(NBOX):

        def send_box(k, carry):
            d = (w + k) % WIDE
            remote(sbuf[c].at[k], rbuf[c].at[w], boxsend.at[c], boxrecv.at[c], (d, z)).start()
            return carry

        lax.fori_loop(1, WIDE, send_box, 0)
    all_facts = remote(
        message.at[pl.ds(0, PEERS)], frecv.at[pl.ds(0, PEERS)], factsem.at[0], factsem.at[1],
        ((w + 1) % WIDE, z),
    )
    all_facts.wait_recv()
    down = pltpu.make_async_copy(frecv, fsm, fsem)
    down.start()
    down.wait()

    def scan(s, carry):
        count, picks = carry
        live = fsm[s, 0, LIVE]
        place_s[s] = jnp.minimum(count, OWNED - 1)
        picks = tuple(jnp.where((live > 0) & (count == p), s, picks[p]) for p in range(OWNED))
        return count + live, picks

    _, picks = lax.fori_loop(
        0, WIDE, scan, (jnp.int32(0), tuple(jnp.int32(0) for _ in range(OWNED)))
    )
    for p in range(OWNED):
        pick_s[p] = picks[p]
        facts8[p : p + 1, :] = frecv[picks[p]]

    def known(p, which):
        return fsm[pick_s[p], 0, which]

    def spread_z(c, quarter, k, to):
        r0, nr, c0, nc = BOXES[c]
        where = crop.at[quarter, :, pl.ds(r0, nr), pl.ds(c0, nc)]
        return remote(where, where, zsend.at[c, k], zrecv.at[c, k], (w, to))

    all_boxes = []
    z_sent = []
    for c, (r0, nr, c0, nc) in enumerate(BOXES):
        boxes = remote(
            sbuf[c].at[pl.ds(0, PEERS)], rbuf[c].at[pl.ds(0, PEERS)], boxsend.at[c],
            boxrecv.at[c], ((w + 1) % WIDE, z),
        )
        all_boxes.append(boxes)
        boxes.wait_recv()
        for p in range(OWNED):
            crop[z, p, r0 : r0 + nr, c0 : c0 + nc] = rbuf[c][picks[p]]
        for k in (2, 1, 3):
            z_sent.append(spread_z(c, z, k, (z + k) % NARROW))
            z_sent[-1].start()
    for c in range(NBOX):
        for k in range(1, NARROW):
            s = (z + NARROW - k) % NARROW
            spread_z(c, s, k, s).wait_recv()

    diag = head_diag()
    ones = jnp.where(diag, 1.0, 0.0).astype(BF)
    row48 = iota((SPAN, QROWS), 0)
    col48 = iota((SPAN, QROWS), 1)
    for p in range(OWNED):
        start = known(p, START)
        length = known(p, LEN)
        rows = pl.ds(p * SPAN, SPAN)
        source = row48 + start
        alive = row48 < length
        top = jnp.where((col48 == source) & alive, 1.0, 0.0).astype(BF)
        low = jnp.where((col48 + QROWS == source) & alive, 1.0, 0.0).astype(BF)
        lhs = mm(top, crop[0, p]) + mm(low, crop[2, p])
        rhs = mm(top, crop[1, p]) + mm(low, crop[3, p])
        square = jnp.sum(lhs * lhs, axis=1, keepdims=True) + jnp.sum(
            rhs * rhs, axis=1, keepdims=True
        )
        inv = lax.rsqrt(square * (1.0 / D) + EPS)
        normed[rows, 0:QCOLS] = (lhs * inv).astype(BF)
        normed[rows, QCOLS:D] = (rhs * inv).astype(BF)
        inv_tokens[rows, :] = jnp.broadcast_to(inv, (SPAN, 128))
        scale = length.astype(F32)
        pooled[p : p + 1, 0:QCOLS] = jnp.sum(lhs, axis=0, keepdims=True) / scale
        pooled[p : p + 1, QCOLS:D] = jnp.sum(rhs, axis=0, keepdims=True) / scale
    load_qkv.wait()
    load_out.wait()
    for j in range(9):
        cols = pl.ds(j * GROUP, GROUP)
        mixed = mm(normed[...], wqkv[:, cols])
        if j < 6:
            square = mm((mixed * mixed).astype(BF), ones)
            inv = lax.rsqrt(square * (1.0 / HEAD) + EPS)
            qkv[:, cols] = (mixed * inv).astype(BF)
            inv_heads[:, cols] = inv.astype(BF)
        else:
            qkv[:, cols] = mixed.astype(BF)

    ones_lane = iota((1, GROUP), 1) % SPAN
    query_block = ones_lane // 16
    key_row = iota((SPAN, GROUP), 0)
    key_block = key_row // 16
    causal = key_row <= ones_lane

    def attend(p):
        rows = pl.ds(pl.multiple_of(p * SPAN, SPAN), SPAN)
        length = known(p, LEN)
        listed = None
        for j in range(4):
            want = [known(p, BLOCKS + 4 * b + j) for b in range(4)]
            want = jnp.where(
                query_block < 2,
                jnp.where(query_block == 0, want[0], want[1]),
                jnp.where(query_block == 2, want[2], want[3]),
            )
            hit = key_block == want
            listed = hit if listed is None else listed | hit
        allowed = jnp.where(listed & causal, 1.0, 0.0)
        alive = jnp.where(ones_lane < length, 1.0, 0.0)
        scale = length.astype(F32)
        for g in range(3):
            cols = pl.ds(g * GROUP, GROUP)
            query = spread_heads(qkv[rows, cols], diag)
            keys = qkv[rows, pl.ds(D + g * GROUP, GROUP)]
            weight = jnp.exp(mm_t(keys, query) * (4.0 / HEAD)) * allowed
            total = jnp.sum(weight, axis=0, keepdims=True)
            prob = (weight * (alive / total)).astype(BF)
            probs[p, :, cols] = prob
            column = mm(prob, ones) / scale
            col_w[rows, cols] = column
            values = qkv[rows, pl.ds(2 * D + g * GROUP, GROUP)].astype(F32)
            mean_att[pl.ds(p, 1), cols] = jnp.sum(column * values, axis=0, keepdims=True)

    def attend_some(i, carry):
        for q in range(PAIR):
            attend(i * PAIR + q)
        return carry

    lax.fori_loop(0, OWNED // PAIR, attend_some, 0)
    att_hi, att_lo = split_hi_lo(mean_att[...])
    pooled[...] += mm(att_hi, wout[...]) + mm(att_lo, wout[...])

    pool = pooled[...]
    inv_pool = lax.rsqrt(jnp.sum(pool * pool, axis=1, keepdims=True) + EPS)
    embed = pool * inv_pool
    mine[:, 0:D] = embed
    mine[:, D : D + 128] = jnp.broadcast_to(facts8[:, OFF : OFF + 1].astype(F32), (OWNED, 128))
    e_copies = []
    for k in range(1, NARROW):
        copy = remote(
            mine, everyone.at[z], esend.at[k], erecv.at[k], (w, (z + k) % NARROW)
        )
        copy.start()
        e_copies.append(copy)
    everyone[z] = mine[...]
    normed_t[...] = normed[...].T
    for k in range(1, NARROW):
        s = (z + NARROW - k) % NARROW
        remote(mine, everyone.at[s], esend.at[k], erecv.at[k], (w, s)).wait_recv()
    total = NARROW * OWNED
    full = everyone[...].reshape(total, D + 128)
    group = full[:, 0:D]
    offset = full[:, D : D + total].astype(I32)
    high = lax.Precision.HIGHEST
    logit = (
        lax.dot_general(
            group, group, (((1,), (1,)), ((), ())), precision=high, preferred_element_type=F32
        )
        / 0.1
    )
    row = iota((total, total), 0)
    col = iota((total, total), 1)
    positive = ((row // OWNED + offset) % NARROW) * OWNED + row % OWNED
    weight = jnp.where(row != col, jnp.exp(logit), 0.0)
    prob = weight / jnp.sum(weight, axis=1, keepdims=True)
    coef = (512.0 / 0.1) * (prob - jnp.where(col == positive, 1.0, 0.0))
    d_embed[...] = jnp.dot(
        coef, group, precision=high, preferred_element_type=F32
    ) + lax.dot_general(
        coef, group, (((0,), (0,)), ((), ())), precision=high, preferred_element_type=F32
    )
    own = d_embed[pl.ds(pl.multiple_of(OWNED * z, OWNED), OWNED), :]
    d_pooled[...] = inv_pool * (own - embed * jnp.sum(own * embed, axis=1, keepdims=True))

    hi, lo = split_hi_lo(d_pooled[...])
    d_att[...] = mm_t(hi, wout[...]) + mm_t(lo, wout[...])
    other = w + 1 - 2 * core
    w_sent = []

    def put_dw(t, j, got):
        dw[t, :, :, :, pl.ds(j * GROUP, GROUP)] = got.reshape(16, 2, WROWS, GROUP).astype(BF)

    def cross(t):
        return remote(dw.at[t, :, 1 - core], core_in.at[t], csend.at[t], crecv.at[t], (other, z))

    def along(t, first, k):
        if (t in (0, 3)) == first:
            return ((y * CHIP_X + (x + k) % CHIP_X) * 2 + core, z), (x + k) % CHIP_X
        return ((((y + k) % CHIP_Y) * CHIP_X + x) * 2 + core, z), (y + k) % CHIP_Y

    def start_cross(t):
        w_sent.append(cross(t))
        w_sent[-1].start()

    def start_first(t):
        cross(t).wait_recv()

        def pair(i, carry):
            at = (i % CHIP_X, i // CHIP_X) if t in (0, 3) else (i // CHIP_X, i % CHIP_X)
            acc[t, at[0], at[1]] = (
                dw[t, i, core].astype(F32) + core_in[t, i].astype(F32)
            ).astype(BF)
            return carry

        lax.fori_loop(0, CHIP_X * CHIP_Y, pair, 0)
        for k in (2, 1, 3):
            to, at = along(t, True, k)
            w_sent.append(
                remote(acc.at[t, at], ring.at[t, k], asend.at[t, k], arecv.at[t, k], to)
            )
            w_sent[-1].start()

    def start_second(t):
        for k in range(1, 4):
            to, at = along(t, True, k)
            remote(acc.at[t, at], ring.at[t, k], asend.at[t, k], arecv.at[t, k], to).wait_recv()
        here = along(t, True, 0)[1]

        def middle(i, carry):
            mid[t, i] = (
                (acc[t, here, i].astype(F32) + ring[t, 1, i].astype(F32))
                + (ring[t, 2, i].astype(F32) + ring[t, 3, i].astype(F32))
            ).astype(BF)
            return carry

        lax.fori_loop(0, 4, middle, 0)
        for k in (2, 1, 3):
            to, at = along(t, False, k)
            w_sent.append(
                remote(mid.at[t, at], ends.at[t, k], a2send.at[t, k], a2recv.at[t, k], to)
            )
            w_sent[-1].start()

    def finish_second(t):
        for k in range(1, 4):
            to, at = along(t, False, k)
            remote(mid.at[t, at], ends.at[t, k], a2send.at[t, k], a2recv.at[t, k], to).wait_recv()
        here = along(t, False, 0)[1]
        final[0:WROWS, t * D : (t + 1) * D] = (
            mid[t, here].astype(F32) + ends[t, 1].astype(F32)
        ) + (ends[t, 2].astype(F32) + ends[t, 3].astype(F32))

    both = jnp.concatenate([att_hi, att_lo], axis=0)
    twice = jnp.concatenate([hi, hi], axis=0)
    for j in range(3):
        put_dw(3, j, mm_l(both, twice[:, j * GROUP : (j + 1) * GROUP]))
    start_cross(3)
    for p in range(OWNED):
        rows = pl.ds(p * SPAN, SPAN)
        g_mixed[rows, 2 * D : 3 * D] = (col_w[rows, :] * d_att[p : p + 1, :]).astype(BF)
    for j in range(3):
        put_dw(2, j, mm(normed_t[...], g_mixed[:, pl.ds(2 * D + j * GROUP, GROUP)]))
    start_cross(2)
    start_first(3)

    def attend_back(p):
        rows = pl.ds(pl.multiple_of(p * SPAN, SPAN), SPAN)
        scale = known(p, LEN).astype(F32)
        for g in range(3):
            cols = pl.ds(g * GROUP, GROUP)
            kcols = pl.ds(D + g * GROUP, GROUP)
            query = spread_heads(qkv[rows, cols], diag)
            keys = qkv[rows, kcols]
            values = qkv[rows, pl.ds(2 * D + g * GROUP, GROUP)].astype(F32)
            d_row = d_att[pl.ds(p, 1), cols] / scale
            slope = mm((values * d_row).astype(BF), ones)
            prob = probs[p, :, cols].astype(F32)
            tilted = prob * slope
            center = jnp.sum(tilted, axis=0, keepdims=True)
            d_score = ((tilted - prob * center) * (4.0 / HEAD)).astype(BF)
            g_mixed[rows, kcols] = mm(d_score, query).astype(BF)
            g_mixed[rows, cols] = gather_heads(mm_l(d_score, keys), diag).astype(BF)

    def attend_back_some(i, carry):
        for q in range(PAIR):
            attend_back(i * PAIR + q)
        return carry

    lax.fori_loop(0, OWNED // PAIR // 2, attend_back_some, 0)
    start_first(2)
    lax.fori_loop(OWNED // PAIR // 2, OWNED // PAIR, attend_back_some, 0)
    for j in range(6):
        cols = pl.ds(j * GROUP, GROUP)
        unit = qkv[:, cols].astype(F32)
        grad = g_mixed[:, cols].astype(F32)
        mean = mm((grad * unit).astype(BF), ones) * (1.0 / HEAD)
        g_mixed[:, cols] = (inv_heads[:, cols].astype(F32) * (grad - unit * mean)).astype(BF)
    for j in range(3):
        cols = pl.ds(j * GROUP, GROUP)
        d_normed[:, cols] = mm_t(g_mixed[...], wqkv[cols, :])
    for p in range(OWNED):
        rows = pl.ds(p * SPAN, SPAN)
        length = known(p, LEN)
        unit = normed[rows, :].astype(F32)
        grad = d_normed[rows, :]
        mean = jnp.sum(grad * unit, axis=1, keepdims=True) * (1.0 / D)
        back = inv_tokens[rows, 0:1] * (grad - unit * mean)
        back = back + d_pooled[p : p + 1, :] / length.astype(F32)
        alive = iota((SPAN, D), 0) < length
        d_tokens[rows, :] = jnp.where(alive, back, 0.0).astype(BF)

    h_sent = []
    shift = iota((HIST, SPAN), 0) - iota((HIST, SPAN), 1)
    puts = [jnp.where(shift == known(p, START), 1.0, 0.0).astype(BF) for p in range(OWNED)]
    for c, (c0, nc) in enumerate(BACKS):
        for p in range(OWNED):
            spread = mm(puts[p], d_tokens[p * SPAN : (p + 1) * SPAN, c0 : c0 + nc])
            for j in range(NARROW):
                d_hist[c][j, p] = spread[j * ORROWS : (j + 1) * ORROWS].astype(BF)
        for k in (2, 1, 3):
            t = (z + k) % NARROW
            h_sent.append(remote(d_hist[c].at[t], zin[c].at[k], hsend.at[c, k], hrecv.at[c, k], (w, t)))
            h_sent[-1].start()
    for t in (0, 1):
        for j in range(3):
            put_dw(t, j, mm(normed_t[...], g_mixed[:, pl.ds(t * D + j * GROUP, GROUP)]))
        start_cross(t)
    start_second(3)
    start_second(2)
    start_first(0)
    start_first(1)
    all_back = []
    for c, (c0, nc) in enumerate(BACKS):
        for k in range(1, NARROW):
            s = (z + NARROW - k) % NARROW
            remote(d_hist[c].at[s], zin[c].at[k], hsend.at[c, k], hrecv.at[c, k], (w, s)).wait_recv()
        for p in range(OWNED):
            dsum[c][p] = (
                (d_hist[c][z, p].astype(F32) + zin[c][1, p].astype(F32))
                + (zin[c][2, p].astype(F32) + zin[c][3, p].astype(F32))
            ).astype(BF)

        def send_back(k, carry):
            d = (w + k) % WIDE
            sback[c][k] = dsum[c][place_s[d]]
            remote(sback[c].at[k], rback[c].at[w], backsend.at[c], backrecv.at[c], (d, z)).start()
            return carry

        lax.fori_loop(1, WIDE, send_back, 0)
        rback[c][w] = dsum[c][place_s[w]]
        all_back.append(
            remote(
                sback[c].at[pl.ds(0, PEERS)], rback[c].at[pl.ds(0, PEERS)], backsend.at[c],
                backrecv.at[c], ((w + 1) % WIDE, z),
            )
        )
        if c == 1:
            start_second(0)
            start_second(1)
    final[WROWS : WROWS + 8, :] = jnp.zeros((8, WCOLS), F32)
    for t in (3, 2, 0, 1):
        finish_second(t)
    for j in range(NARROW):
        zbuf[j] = final[6 * j : 6 * j + 8, :]
    last = []
    for k in range(1, NARROW):
        t = (z + k) % NARROW
        copy = remote(zbuf.at[t], zlast.at[k], lsend.at[k], lrecv.at[k], (w, t))
        copy.start()
        last.append(copy)
    for c, (c0, nc) in enumerate(BACKS):
        all_back[c].wait_recv()

        def write(a, carry):
            owner = dest[a]
            got = rback[c][jnp.maximum(owner, 0)].astype(F32)
            kept = jnp.where(jnp.full((ORROWS, nc), owner, I32) >= 0, got, 0.0)
            out_hist[a, :, c0 : c0 + nc] = kept.astype(BF)
            return carry

        lax.fori_loop(0, SLOTS, write, 0)
    for copy in last:
        copy.wait_recv()
    out_w[...] = (zbuf[z] + zlast[1]) + (zlast[2] + zlast[3])

    all_facts.wait_send()
    for copy in all_boxes + z_sent + e_copies + w_sent + last + h_sent + all_back:
        copy.wait_send()


def finish_kernel(hist, d_w, out_hist, out_qkv, out_out):
    out_hist[...] = hist[...].astype(F32)
    out_qkv[...] = d_w[0:6, 0 : 3 * D]
    out_out[...] = d_w[0:6, 3 * D : WCOLS]


VM = pl.BlockSpec(memory_space=pltpu.VMEM)
SM = pl.BlockSpec(memory_space=pltpu.SMEM)
HB = pl.BlockSpec(memory_space=pl.ANY)
DMA = pltpu.SemaphoreType.DMA


def vmem(kind, *dims):
    return pltpu.VMEM(dims, kind)


def on_device(
    history, w_qkv, w_out, dest_owner, view_start, view_length, block_list, positive_offset
):
    d_history, d_w = pl.pallas_call(
        whole_kernel,
        out_shape=(
            jax.ShapeDtypeStruct((SLOTS, ORROWS, D), BF),
            jax.ShapeDtypeStruct((8, WCOLS), F32),
        ),
        in_specs=[SM, VM, VM, VM, VM, HB, HB, HB],
        out_specs=(VM, VM),
        scratch_shapes=[
            vmem(BF, D, 3 * D),
            vmem(BF, D, D),
            vmem(I32, 128, 128),
            vmem(I32, 128, 128),
            pltpu.SMEM((WIDE,), I32),
            vmem(I32, WIDE, 1, 128),
            vmem(I32, WIDE, 1, 128),
            pltpu.SMEM((WIDE, 1, 128), I32),
            pltpu.SMEM((OWNED,), I32),
            pltpu.SMEM((WIDE,), I32),
            vmem(I32, OWNED, 128),
            vmem(BF, SLOTS, QROWS, QCOLS),
            vmem(BF, NARROW, OWNED, QROWS, QCOLS),
            vmem(BF, ROWS, D),
            vmem(BF, D, ROWS),
            vmem(BF, ROWS, 3 * D),
            vmem(BF, ROWS, 2 * D),
            vmem(F32, ROWS, 128),
            vmem(BF, OWNED, SPAN, D),
            vmem(F32, ROWS, D),
            vmem(F32, OWNED, D),
            vmem(F32, OWNED, D),
            vmem(F32, OWNED, D + 128),
            vmem(F32, NARROW, OWNED, D + 128),
            vmem(F32, NARROW * OWNED, D),
            vmem(F32, OWNED, D),
            vmem(F32, OWNED, D),
            vmem(BF, ROWS, 3 * D),
            vmem(F32, ROWS, D),
            vmem(BF, ROWS, D),
            vmem(BF, 4, 16, 2, WROWS, D),
            vmem(BF, 4, 16, WROWS, D),
            vmem(BF, 4, 4, 4, WROWS, D),
            vmem(BF, 4, 4, 4, WROWS, D),
            vmem(BF, 4, 4, WROWS, D),
            vmem(BF, 4, 4, WROWS, D),
            vmem(F32, WROWS + 8, WCOLS),
            vmem(F32, NARROW, 8, WCOLS),
            vmem(F32, NARROW, 8, WCOLS),
            *[vmem(BF, WIDE, nr, nc) for _, nr, _, nc in BOXES],
            *[vmem(BF, WIDE, nr, nc) for _, nr, _, nc in BOXES],
            *[vmem(BF, NARROW, OWNED, ORROWS, nc) for _, nc in BACKS],
            *[vmem(BF, NARROW, OWNED, ORROWS, nc) for _, nc in BACKS],
            *[vmem(BF, OWNED, ORROWS, nc) for _, nc in BACKS],
            *[vmem(BF, WIDE, ORROWS, nc) for _, nc in BACKS],
            *[vmem(BF, WIDE, ORROWS, nc) for _, nc in BACKS],
            DMA((2,)), DMA, DMA, DMA((2,)),
            DMA((NBOX,)), DMA((NBOX,)),
            DMA((NBOX, 4)), DMA((NBOX, 4)),
            DMA((NARROW,)), DMA((NARROW,)),
            DMA((4,)), DMA((4,)),
            DMA((4, 4)), DMA((4, 4)),
            DMA((4, 4)), DMA((4, 4)),
            DMA((NARROW,)), DMA((NARROW,)),
            DMA((NBACK, 4)), DMA((NBACK, 4)),
            DMA((NBACK,)), DMA((NBACK,)),
        ],
        compiler_params=pltpu.CompilerParams(
            collective_id=0, has_side_effects=True, vmem_limit_bytes=VMEM_LIMIT
        ),
        name="step",
    )(
        dest_owner, view_start.T, view_length.T, positive_offset.T,
        block_list.reshape(SLOTS, 16).T, history, w_qkv, w_out,
    )
    return pl.pallas_call(
        finish_kernel,
        out_shape=(
            jax.ShapeDtypeStruct((SLOTS, ORROWS, D), F32),
            jax.ShapeDtypeStruct((6, 3 * D), F32),
            jax.ShapeDtypeStruct((6, D), F32),
        ),
        in_specs=[VM, VM],
        out_specs=(VM, VM, VM),
        name="finish",
    )(d_history, d_w)


def solution(mesh):
    return jax.shard_map(
        on_device,
        mesh=mesh,
        in_specs=(
            P("wide", None, None),
            P(),
            P(),
            P("wide"),
            P("wide", "narrow"),
            P("wide", "narrow"),
            P("wide", "narrow", None, None),
            P("wide", "narrow"),
        ),
        out_specs=(
            P("wide", "narrow", None),
            P(("wide", "narrow"), None),
            P(("wide", "narrow"), None),
        ),
        check_vma=False,
    )
```

time: 116 us -> 98.8 us (0.85)
  Pallas kernels: 109 us -> 98 us
  local copies, waits for them, and re-layouts: 2.87 us -> 0 us
  other arithmetic: 2.15 us -> 0 us
    pallas_call x1, Pallas kernels: 109 us -> 95.8 us  [on_device(): pl.pallas_call(whole_kernel, out_shape=(jax.ShapeDtypeStruct((SLOTS, ORRO...]
    slice x2 -> x0, local copies, waits for them, and re-layouts: 2.87 us -> none  [on_device(): return (d_history.astype(F32), d_w[0:6, 0:3 * D], d_w[0:6, 3 * D:WCOLS])]
    pallas_call x0 -> x1, Pallas kernels: none -> 2.17 us  [on_device(): pl.pallas_call(finish_kernel, out_shape=(jax.ShapeDtypeStruct((SLOTS, ORR...]
    convert_element_type x1 -> x0, other arithmetic: 2.15 us -> none  [on_device(): return (d_history.astype(F32), d_w[0:6, 0:3 * D], d_w[0:6, 3 * D:WCOLS])]
where the time goes in v3:
time: 98.8 us; the launch traced here: 98.6 us
  Pallas kernels  98 us (99%)
    pallas_call x1, Pallas kernels, on_device(): pl.pallas_call(whole_kernel, out_shape=(jax.ShapeDtypeStruct((SLOTS, ORRO...  95.8 us
    pallas_call x1, Pallas kernels, on_device(): pl.pallas_call(finish_kernel, out_shape=(jax.ShapeDtypeStruct((SLOTS, ORR...  2.17 us

profile of v3, /device:TPU:0, one launch (start us, length us, event | category | flops | bytes accessed | tf_op | source)
XLA Modules:
  0.0 98.6 jit_solution(8354303903690544384)
XLA Ops:
  0.6 95.8 %step.1 = (bf16[16,24,768]{2,1,0:T(8,128)(2,1)}, f32[8,3072]{1,0:T(8,128)}) custom-call(s32[16]{0:T(128)} %dest.1, s32[1,16]{1,0:T(1,128)} %bitcast.7, s32[1,16]{1,0:T(1,128)} %bitcast.8, s32[1,16]{1,0:T(1,128)} %bitcast.9, s32[16,16]{1,0:T(8,128)} %bitcast.6, bf16[16,96,768]{2,1,0:T(8,128)(2,1)} %hist.1, bf16[768,2304]{1,0:T(8,128)(2,1)} %wqkv_hbm.1, ...), custom_call_target="tpu_custom_call" | custom-call | tf_op jit(solution)/shard_map/step/pallas_call | solution.py:577
  96.5 2.2 %finish.1 = (f32[16,24,768]{2,1,0:T(8,128)}, f32[6,2304]{1,0:T(8,128)}, f32[6,768]{1,0:T(8,128)}) custom-call(bf16[16,24,768]{2,1,0:T(8,128)(2,1)} %get-tuple-element.5.hist, f32[8,3072]{1,0:T(8,128)} %get-tuple-element.6.d_w), custom_call_target="tpu_custom_call" | custom-call | tf_op jit(solution)/shard_map/finish/pallas_call | solution.py:651

commit v4 on v3

--- a/solution.py
+++ b/solution.py
@@ -29,11 +29,17 @@
 WCOLS = 4 * D
 
 LIVE, LEN, OFF, START, BLOCKS = 0, 1, 2, 3, 8
-BOXES = ((0, 16, 0, 384), (16, 16, 0, 384), (32, 16, 0, 256), (32, 16, 256, 128))
+BOXES = (
+    (0, 16, 0, 128, False),
+    (0, 16, 128, 256, False),
+    (16, 16, 0, 384, True),
+    (32, 16, 0, 256, True),
+    (32, 16, 256, 128, False),
+)
 NBOX = len(BOXES)
-BACKS = ((0, 128), (128, 256), (384, 256), (640, 128))
+BACKS = ((0, 128, False), (128, 256, False), (384, 256, False), (640, 128, False))
 NBACK = len(BACKS)
-PAIR = 2
+PAIR = 4
 PEERS = WIDE - 1
 EPS = 1e-06
 VMEM_LIMIT = 60 * 1024 * 1024
@@ -82,8 +88,8 @@
     normed, normed_t, qkv, inv_heads, inv_tokens, probs, col_w, pooled, mean_att,
     mine, everyone, d_embed, d_pooled, d_att, g_mixed, d_normed, d_tokens,
     dw, core_in, acc, ring, mid, ends, final, zbuf, zlast,
-    sbuf_0, sbuf_1, sbuf_2, sbuf_3, rbuf_0, rbuf_1, rbuf_2, rbuf_3,
-    hist_0, hist_1, hist_2, hist_3, zin_0, zin_1, zin_2, zin_3,
+    sbuf_0, sbuf_1, sbuf_2, sbuf_3, sbuf_4, rbuf_0, rbuf_1, rbuf_2, rbuf_3, rbuf_4,
+    hist_0, hist_1, hist_2, hist_3, zin_0, zin_1, zin_2, zin_3, comb_0, comb_1, comb_2, comb_3,
     dsum_0, dsum_1, dsum_2, dsum_3, sback_0, sback_1, sback_2, sback_3,
     rback_0, rback_1, rback_2, rback_3,
     wsem, lsem, fsem, factsem, boxsend, boxrecv, zsend, zrecv, esend, erecv,
@@ -101,10 +107,15 @@
             device_id_type=MESH,
         )
 
-    sbuf = (sbuf_0, sbuf_1, sbuf_2, sbuf_3)
-    rbuf = (rbuf_0, rbuf_1, rbuf_2, rbuf_3)
+    sbuf = (sbuf_0, sbuf_1, sbuf_2, sbuf_3, sbuf_4)
+    rbuf = (rbuf_0, rbuf_1, rbuf_2, rbuf_3, rbuf_4)
     d_hist = (hist_0, hist_1, hist_2, hist_3)
     zin = (zin_0, zin_1, zin_2, zin_3)
+    comb = (comb_0, comb_1, comb_2, comb_3)
+    right = (z + 1) % NARROW
+    left = (z + 3) % NARROW
+    opposite = (z + 2) % NARROW
+    part = OWNED // 2
     dsum = (dsum_0, dsum_1, dsum_2, dsum_3)
     sback = (sback_0, sback_1, sback_2, sback_3)
     rback = (rback_0, rback_1, rback_2, rback_3)
@@ -152,13 +163,13 @@
 
     def fill(k, carry):
         slot = slot_s[(w + k) % WIDE]
-        for c, (r0, nr, c0, nc) in enumerate(BOXES):
+        for c, (r0, nr, c0, nc, ring_z) in enumerate(BOXES):
             sbuf[c][k] = hbuf[slot, r0 : r0 + nr, c0 : c0 + nc]
         return carry
 
     lax.fori_loop(1, WIDE, fill, 0)
     frecv[w] = message[w]
-    for c, (r0, nr, c0, nc) in enumerate(BOXES):
+    for c, (r0, nr, c0, nc, ring_z) in enumerate(BOXES):
         rbuf[c][w] = hbuf[slot_s[w], r0 : r0 + nr, c0 : c0 + nc]
     pl.semaphore_wait(barrier, PEERS + NARROW - 1)
 
@@ -202,14 +213,26 @@
     def known(p, which):
         return fsm[pick_s[p], 0, which]
 
-    def spread_z(c, quarter, k, to):
-        r0, nr, c0, nc = BOXES[c]
-        where = crop.at[quarter, :, pl.ds(r0, nr), pl.ds(c0, nc)]
-        return remote(where, where, zsend.at[c, k], zrecv.at[c, k], (w, to))
+    def hop(c, quarter, lo, size, to, n):
+        r0, nr, c0, nc, _ = BOXES[c]
+        where = crop.at[quarter, pl.ds(lo, size), pl.ds(r0, nr), pl.ds(c0, nc)]
+        return remote(where, where, zsend.at[c, n], zrecv.at[c, n], (w, to))
 
     all_boxes = []
     z_sent = []
-    for c, (r0, nr, c0, nc) in enumerate(BOXES):
+
+    def z_start(copy):
+        copy.start()
+        z_sent.append(copy)
+
+    def pass_on(c):
+        if BOXES[c][4]:
+            hop(c, left, 0, OWNED, left, 0).wait_recv()
+            z_start(hop(c, left, 0, part, right, 2))
+            hop(c, right, 0, OWNED, right, 1).wait_recv()
+            z_start(hop(c, right, part, part, left, 3))
+
+    for c, (r0, nr, c0, nc, ring_z) in enumerate(BOXES):
         boxes = remote(
             sbuf[c].at[pl.ds(0, PEERS)], rbuf[c].at[pl.ds(0, PEERS)], boxsend.at[c],
             boxrecv.at[c], ((w + 1) % WIDE, z),
@@ -218,13 +241,21 @@
         boxes.wait_recv()
         for p in range(OWNED):
             crop[z, p, r0 : r0 + nr, c0 : c0 + nc] = rbuf[c][picks[p]]
-        for k in (2, 1, 3):
-            z_sent.append(spread_z(c, z, k, (z + k) % NARROW))
-            z_sent[-1].start()
-    for c in range(NBOX):
-        for k in range(1, NARROW):
-            s = (z + NARROW - k) % NARROW
-            spread_z(c, s, k, s).wait_recv()
+        if not ring_z:
+            z_start(hop(c, z, 0, OWNED, opposite, 2))
+        z_start(hop(c, z, 0, OWNED, right, 0))
+        z_start(hop(c, z, 0, OWNED, left, 1))
+        if c > 0:
+            pass_on(c - 1)
+    pass_on(NBOX - 1)
+    for c, box in enumerate(BOXES):
+        if box[4]:
+            hop(c, opposite, 0, part, left, 2).wait_recv()
+            hop(c, opposite, part, part, right, 3).wait_recv()
+        else:
+            hop(c, left, 0, OWNED, left, 0).wait_recv()
+            hop(c, right, 0, OWNED, right, 1).wait_recv()
+            hop(c, opposite, 0, OWNED, opposite, 2).wait_recv()
 
     diag = head_diag()
     ones = jnp.where(diag, 1.0, 0.0).astype(BF)
@@ -413,9 +444,24 @@
             to, at = along(t, False, k)
             remote(mid.at[t, at], ends.at[t, k], a2send.at[t, k], a2recv.at[t, k], to).wait_recv()
         here = along(t, False, 0)[1]
-        final[0:WROWS, t * D : (t + 1) * D] = (
-            mid[t, here].astype(F32) + ends[t, 1].astype(F32)
-        ) + (ends[t, 2].astype(F32) + ends[t, 3].astype(F32))
+        final[t, 0:WROWS, :] = (mid[t, here].astype(F32) + ends[t, 1].astype(F32)) + (
+            ends[t, 2].astype(F32) + ends[t, 3].astype(F32)
+        )
+        final[t, WROWS : WROWS + 8, :] = jnp.zeros((8, D), F32)
+        for j in range(NARROW):
+            zbuf[t, j] = final[t, 6 * j : 6 * j + 8, :]
+        for k in (2, 1, 3):
+            d = (z + k) % NARROW
+            w_sent.append(
+                remote(zbuf.at[t, d], zlast.at[t, k], lsend.at[t, k], lrecv.at[t, k], (w, d))
+            )
+            w_sent[-1].start()
+
+    def finish_last(t):
+        for k in range(1, NARROW):
+            d = (z + k) % NARROW
+            remote(zbuf.at[t, d], zlast.at[t, k], lsend.at[t, k], lrecv.at[t, k], (w, d)).wait_recv()
+        out_w[:, t * D : (t + 1) * D] = (zbuf[t, z] + zlast[t, 1]) + (zlast[t, 2] + zlast[t, 3])
 
     both = jnp.concatenate([att_hi, att_lo], axis=0)
     twice = jnp.concatenate([hi, hi], axis=0)
@@ -453,18 +499,24 @@
             attend_back(i * PAIR + q)
         return carry
 
-    lax.fori_loop(0, OWNED // PAIR // 2, attend_back_some, 0)
+    lax.fori_loop(0, 1, attend_back_some, 0)
     start_first(2)
-    lax.fori_loop(OWNED // PAIR // 2, OWNED // PAIR, attend_back_some, 0)
+    lax.fori_loop(1, 2, attend_back_some, 0)
     for j in range(6):
         cols = pl.ds(j * GROUP, GROUP)
         unit = qkv[:, cols].astype(F32)
         grad = g_mixed[:, cols].astype(F32)
         mean = mm((grad * unit).astype(BF), ones) * (1.0 / HEAD)
         g_mixed[:, cols] = (inv_heads[:, cols].astype(F32) * (grad - unit * mean)).astype(BF)
+    for t in (0, 1):
+        for j in range(3):
+            put_dw(t, j, mm(normed_t[...], g_mixed[:, pl.ds(t * D + j * GROUP, GROUP)]))
+        start_cross(t)
     for j in range(3):
         cols = pl.ds(j * GROUP, GROUP)
         d_normed[:, cols] = mm_t(g_mixed[...], wqkv[cols, :])
+    start_first(0)
+    start_first(1)
     for p in range(OWNED):
         rows = pl.ds(p * SPAN, SPAN)
         length = known(p, LEN)
@@ -477,35 +529,94 @@
         d_tokens[rows, :] = jnp.where(alive, back, 0.0).astype(BF)
 
     h_sent = []
+
+    def back_start(copy):
+        copy.start()
+        h_sent.append(copy)
+
+    def h_direct(c, k, quarter, to):
+        return remote(
+            d_hist[c].at[quarter], zin[c].at[k], hsend.at[c, k], hrecv.at[c, k], (w, to)
+        )
+
+    def h_slot(c, slot):
+        return zin[c].at[slot // 2, pl.ds(part * (slot % 2), part)]
+
+    def h_step(c, quarter, lo, n, to):
+        return remote(
+            d_hist[c].at[quarter, pl.ds(lo, part)], h_slot(c, n), hsend.at[c, n],
+            hrecv.at[c, n], (w, to),
+        )
+
+    def h_pass(c, side, to):
+        return remote(
+            comb[c].at[side], h_slot(c, 4 + side), hsend.at[c, 4 + side], hrecv.at[c, 4 + side],
+            (w, to),
+        )
+
+    def h_relay(c):
+        h_step(c, opposite, 0, 0, left).wait_recv()
+        for p in range(part):
+            comb[c][0, p] = (
+                d_hist[c][right, p].astype(F32) + zin[c][0, p].astype(F32)
+            ).astype(BF)
+        back_start(h_pass(c, 0, right))
+        h_step(c, opposite, part, 1, right).wait_recv()
+        for p in range(part):
+            comb[c][1, p] = (
+                d_hist[c][left, part + p].astype(F32) + zin[c][0, part + p].astype(F32)
+            ).astype(BF)
+        back_start(h_pass(c, 1, left))
+
+    def h_collect(c):
+        if not BACKS[c][2]:
+            for k in range(1, NARROW):
+                s = (z + NARROW - k) % NARROW
+                h_direct(c, k, s, s).wait_recv()
+            for p in range(OWNED):
+                dsum[c][p] = (
+                    (d_hist[c][z, p].astype(F32) + zin[c][1, p].astype(F32))
+                    + (zin[c][2, p].astype(F32) + zin[c][3, p].astype(F32))
+                ).astype(BF)
+            return
+        h_step(c, right, part, 2, left).wait_recv()
+        h_step(c, left, 0, 3, right).wait_recv()
+        h_pass(c, 0, left).wait_recv()
+        h_pass(c, 1, right).wait_recv()
+        for p in range(part):
+            dsum[c][p] = (
+                (d_hist[c][z, p].astype(F32) + zin[c][2, p].astype(F32))
+                + zin[c][1, part + p].astype(F32)
+            ).astype(BF)
+            dsum[c][part + p] = (
+                (d_hist[c][z, part + p].astype(F32) + zin[c][2, part + p].astype(F32))
+                + zin[c][1, p].astype(F32)
+            ).astype(BF)
+
     shift = iota((HIST, SPAN), 0) - iota((HIST, SPAN), 1)
     puts = [jnp.where(shift == known(p, START), 1.0, 0.0).astype(BF) for p in range(OWNED)]
-    for c, (c0, nc) in enumerate(BACKS):
+    for c, (c0, nc, ring_z) in enumerate(BACKS):
         for p in range(OWNED):
             spread = mm(puts[p], d_tokens[p * SPAN : (p + 1) * SPAN, c0 : c0 + nc])
             for j in range(NARROW):
                 d_hist[c][j, p] = spread[j * ORROWS : (j + 1) * ORROWS].astype(BF)
-        for k in (2, 1, 3):
-            t = (z + k) % NARROW
-            h_sent.append(remote(d_hist[c].at[t], zin[c].at[k], hsend.at[c, k], hrecv.at[c, k], (w, t)))
-            h_sent[-1].start()
-    for t in (0, 1):
-        for j in range(3):
-            put_dw(t, j, mm(normed_t[...], g_mixed[:, pl.ds(t * D + j * GROUP, GROUP)]))
-        start_cross(t)
+        if ring_z:
+            back_start(h_step(c, opposite, 0, 0, right))
+            back_start(h_step(c, opposite, part, 1, left))
+            back_start(h_step(c, right, part, 2, right))
+            back_start(h_step(c, left, 0, 3, left))
+        else:
+            for k in (2, 1, 3):
+                t = (z + k) % NARROW
+                back_start(h_direct(c, k, t, t))
     start_second(3)
     start_second(2)
-    start_first(0)
-    start_first(1)
     all_back = []
-    for c, (c0, nc) in enumerate(BACKS):
-        for k in range(1, NARROW):
-            s = (z + NARROW - k) % NARROW
-            remote(d_hist[c].at[s], zin[c].at[k], hsend.at[c, k], hrecv.at[c, k], (w, s)).wait_recv()
-        for p in range(OWNED):
-            dsum[c][p] = (
-                (d_hist[c][z, p].astype(F32) + zin[c][1, p].astype(F32))
-                + (zin[c][2, p].astype(F32) + zin[c][3, p].astype(F32))
-            ).astype(BF)
+    for c in range(NBACK):
+        if BACKS[c][2]:
+            h_relay(c)
+    for c, (c0, nc, ring_z) in enumerate(BACKS):
+        h_collect(c)
 
         def send_back(k, carry):
             d = (w + k) % WIDE
@@ -524,18 +635,11 @@
         if c == 1:
             start_second(0)
             start_second(1)
-    final[WROWS : WROWS + 8, :] = jnp.zeros((8, WCOLS), F32)
-    for t in (3, 2, 0, 1):
-        finish_second(t)
-    for j in range(NARROW):
-        zbuf[j] = final[6 * j : 6 * j + 8, :]
-    last = []
-    for k in range(1, NARROW):
-        t = (z + k) % NARROW
-        copy = remote(zbuf.at[t], zlast.at[k], lsend.at[k], lrecv.at[k], (w, t))
-        copy.start()
-        last.append(copy)
-    for c, (c0, nc) in enumerate(BACKS):
+    finish_second(3)
+    finish_second(2)
+    finish_second(0)
+    finish_second(1)
+    for c, (c0, nc, ring_z) in enumerate(BACKS):
         all_back[c].wait_recv()
 
         def write(a, carry):
@@ -546,12 +650,11 @@
             return carry
 
         lax.fori_loop(0, SLOTS, write, 0)
-    for copy in last:
-        copy.wait_recv()
-    out_w[...] = (zbuf[z] + zlast[1]) + (zlast[2] + zlast[3])
+    for t in (3, 2, 0, 1):
+        finish_last(t)
 
     all_facts.wait_send()
-    for copy in all_boxes + z_sent + e_copies + w_sent + last + h_sent + all_back:
+    for copy in all_boxes + z_sent + e_copies + w_sent + h_sent + all_back:
         copy.wait_send()
 
 
@@ -619,16 +722,17 @@
             vmem(BF, 4, 4, 4, WROWS, D),
             vmem(BF, 4, 4, WROWS, D),
             vmem(BF, 4, 4, WROWS, D),
-            vmem(F32, WROWS + 8, WCOLS),
-            vmem(F32, NARROW, 8, WCOLS),
-            vmem(F32, NARROW, 8, WCOLS),
-            *[vmem(BF, WIDE, nr, nc) for _, nr, _, nc in BOXES],
-            *[vmem(BF, WIDE, nr, nc) for _, nr, _, nc in BOXES],
-            *[vmem(BF, NARROW, OWNED, ORROWS, nc) for _, nc in BACKS],
-            *[vmem(BF, NARROW, OWNED, ORROWS, nc) for _, nc in BACKS],
-            *[vmem(BF, OWNED, ORROWS, nc) for _, nc in BACKS],
-            *[vmem(BF, WIDE, ORROWS, nc) for _, nc in BACKS],
-            *[vmem(BF, WIDE, ORROWS, nc) for _, nc in BACKS],
+            vmem(F32, 4, WROWS + 8, D),
+            vmem(F32, 4, NARROW, 8, D),
+            vmem(F32, 4, NARROW, 8, D),
+            *[vmem(BF, WIDE, nr, nc) for _, nr, _, nc, _ in BOXES],
+            *[vmem(BF, WIDE, nr, nc) for _, nr, _, nc, _ in BOXES],
+            *[vmem(BF, NARROW, OWNED, ORROWS, nc) for _, nc, _ in BACKS],
+            *[vmem(BF, NARROW, OWNED, ORROWS, nc) for _, nc, _ in BACKS],
+            *[vmem(BF, 2, OWNED // 2, ORROWS, nc) for _, nc, _ in BACKS],
+            *[vmem(BF, OWNED, ORROWS, nc) for _, nc, _ in BACKS],
+            *[vmem(BF, WIDE, ORROWS, nc) for _, nc, _ in BACKS],
+            *[vmem(BF, WIDE, ORROWS, nc) for _, nc, _ in BACKS],
             DMA((2,)), DMA, DMA, DMA((2,)),
             DMA((NBOX,)), DMA((NBOX,)),
             DMA((NBOX, 4)), DMA((NBOX, 4)),
@@ -636,8 +740,8 @@
             DMA((4,)), DMA((4,)),
             DMA((4, 4)), DMA((4, 4)),
             DMA((4, 4)), DMA((4, 4)),
-            DMA((NARROW,)), DMA((NARROW,)),
-            DMA((NBACK, 4)), DMA((NBACK, 4)),
+            DMA((4, 4)), DMA((4, 4)),
+            DMA((NBACK, 6)), DMA((NBACK, 6)),
             DMA((NBACK,)), DMA((NBACK,)),
         ],
         compiler_params=pltpu.CompilerParams(

time: 98.8 us -> 94.2 us (0.953); the launches traced: 98.6 us -> 93 us
  Pallas kernels: 98 us -> 92.3 us
    pallas_call x1, Pallas kernels: 95.8 us -> 90.2 us  [on_device(): pl.pallas_call(whole_kernel, out_shape=(jax.ShapeDtypeStruct((SLOTS, ORRO...]
where the time goes in v4:
time: 94.2 us; the launch traced here: 93 us
  Pallas kernels  92.3 us (98%)
    pallas_call x1, Pallas kernels, on_device(): pl.pallas_call(whole_kernel, out_shape=(jax.ShapeDtypeStruct((SLOTS, ORRO...  90.2 us
    pallas_call x1, Pallas kernels, on_device(): pl.pallas_call(finish_kernel, out_shape=(jax.ShapeDtypeStruct((SLOTS, ORR...  2.17 us

profile of v4, /device:TPU:0, one launch (start us, length us, event | category | flops | bytes accessed | tf_op | source)
XLA Modules:
  0.0 93.0 jit_solution(8481882753722220242)
XLA Ops:
  0.6 90.2 %step.1 = (bf16[16,24,768]{2,1,0:T(8,128)(2,1)}, f32[8,3072]{1,0:T(8,128)}) custom-call(s32[16]{0:T(128)} %dest.1, s32[1,16]{1,0:T(1,128)} %bitcast.7, s32[1,16]{1,0:T(1,128)} %bitcast.8, s32[1,16]{1,0:T(1,128)} %bitcast.9, s32[16,16]{1,0:T(8,128)} %bitcast.6, bf16[16,96,768]{2,1,0:T(8,128)(2,1)} %hist.1, bf16[768,2304]{1,0:T(8,128)(2,1)} %wqkv_hbm.1, ...), custom_call_target="tpu_custom_call" | custom-call | tf_op jit(solution)/shard_map/step/pallas_call | solution.py:680
  90.8 2.2 %finish.1 = (f32[16,24,768]{2,1,0:T(8,128)}, f32[6,2304]{1,0:T(8,128)}, f32[6,768]{1,0:T(8,128)}) custom-call(bf16[16,24,768]{2,1,0:T(8,128)(2,1)} %get-tuple-element.5.hist, f32[8,3072]{1,0:T(8,128)} %get-tuple-element.6.d_w), custom_call_target="tpu_custom_call" | custom-call | tf_op jit(solution)/shard_map/finish/pallas_call | solution.py:755

commit v5 on v4

--- a/solution.py
+++ b/solution.py
@@ -637,9 +637,10 @@
             start_second(1)
     finish_second(3)
     finish_second(2)
-    finish_second(0)
-    finish_second(1)
     for c, (c0, nc, ring_z) in enumerate(BACKS):
+        if c == 2:
+            finish_second(0)
+            finish_second(1)
         all_back[c].wait_recv()
 
         def write(a, carry):

time: 94.2 us -> 94.2 us (level)
  no operation moved by 1% of the time
where the time goes in v5:
time: 94.2 us; the launch traced here: 93 us
  Pallas kernels  92.3 us (98%)
    pallas_call x1, Pallas kernels, on_device(): pl.pallas_call(whole_kernel, out_shape=(jax.ShapeDtypeStruct((SLOTS, ORRO...  90.2 us
    pallas_call x1, Pallas kernels, on_device(): pl.pallas_call(finish_kernel, out_shape=(jax.ShapeDtypeStruct((SLOTS, ORR...  2.17 us

profile of v5, /device:TPU:0, one launch (start us, length us, event | category | flops | bytes accessed | tf_op | source)
XLA Modules:
  0.0 93.0 jit_solution(6122666057521786394)
XLA Ops:
  0.6 90.2 %step.1 = (bf16[16,24,768]{2,1,0:T(8,128)(2,1)}, f32[8,3072]{1,0:T(8,128)}) custom-call(s32[16]{0:T(128)} %dest.1, s32[1,16]{1,0:T(1,128)} %bitcast.7, s32[1,16]{1,0:T(1,128)} %bitcast.8, s32[1,16]{1,0:T(1,128)} %bitcast.9, s32[16,16]{1,0:T(8,128)} %bitcast.6, bf16[16,96,768]{2,1,0:T(8,128)(2,1)} %hist.1, bf16[768,2304]{1,0:T(8,128)(2,1)} %wqkv_hbm.1, ...), custom_call_target="tpu_custom_call" | custom-call | tf_op jit(solution)/shard_map/step/pallas_call | solution.py:681
  90.8 2.2 %finish.1 = (f32[16,24,768]{2,1,0:T(8,128)}, f32[6,2304]{1,0:T(8,128)}, f32[6,768]{1,0:T(8,128)}) custom-call(bf16[16,24,768]{2,1,0:T(8,128)(2,1)} %get-tuple-element.5.hist, f32[8,3072]{1,0:T(8,128)} %get-tuple-element.6.d_w), custom_call_target="tpu_custom_call" | custom-call | tf_op jit(solution)/shard_map/finish/pallas_call | solution.py:756
